TPU v7x, 256 devices: a whole 4x4x8 slice. The times are simulated.
256 devices in a mesh: batch: 16 (over z, y_hi), group: 16 (over y_lo, x, core).
Axes of the slice: x: 4, y: 4 (y_hi: 2, y_lo: 2; y = y_hi * 2 + y_lo), z: 8, core: 2. Of those that a mesh axis runs over, the one named last changes fastest.
Arguments:
- picture_embeds: bfloat16 [16384, 1152], P(('batch', 'group'))
- caption_embeds: bfloat16 [16384, 1152], P(('batch', 'group'))
- positive_caption_ids: int32 [16384], P(('batch', 'group')), may hold values from 0 to 16383, as said below
- logit_multiplier: float32 [1], replicated, may hold values from 11 to 16
- logit_shift: float32 [1], replicated, may hold values from -0.5 to 0.5
Outputs:
- image_grad_t: bfloat16 [1152, 16384], P('group', 'batch')
- text_grad: float32 [16384, 1152], P(('batch', 'group'))
Inputs may be any that keep to these rules, and one draw needn't show every extreme that they name: `positive_caption_ids`: labels is a permutation: each text is the positive of exactly one image.
All inputs are finite; a program needn't handle non-finite values.
Results may differ from a plain program's by a relative error of at most 0.008.
Values may be sent and summed in bfloat16 or wider, within the bound.
A program may use at most 64 MiB of HBM per device.

v0:
```python
import jax
import jax.numpy as jnp
from jax import lax
from jax.sharding import PartitionSpec as P

epsilon = 1e-06


def shifted(shard, axis, by):
    size = lax.axis_size(axis)
    return lax.ppermute(shard, axis, [(i, (i + by) % size) for i in range(size)])


def unit_rows(values):
    wide = values.astype(jnp.float32)
    inverse = lax.rsqrt(jnp.sum(wide * wide, axis=1, keepdims=True) + epsilon)
    return (wide * inverse, inverse)


def tile_loss_entries(
    picture_unit_vectors,
    picture_class_ids,
    caption_slice,
    caption_count,
    multiplier_scalar,
    shift_scalar,
):
    cross_cosine_grid = lax.dot_general(
        picture_unit_vectors,
        caption_slice,
        (((1,), (1,)), ((), ())),
        preferred_element_type=jnp.float32,
    )
    cross_raw_similarity = multiplier_scalar * cross_cosine_grid + shift_scalar
    match_polarity = jnp.where(
        picture_class_ids[:, None] == caption_count[None, :], 1.0, -1.0
    ).astype(jnp.float32)
    entry_factor = (
        multiplier_scalar * -match_polarity * jax.nn.sigmoid(-match_polarity * cross_raw_similarity)
    ).astype(jnp.bfloat16)
    into_image = jnp.dot(entry_factor, caption_slice, preferred_element_type=jnp.float32)
    into_text = lax.dot_general(
        entry_factor,
        picture_unit_vectors,
        (((0,), (0,)), ((), ())),
        preferred_element_type=jnp.float32,
    )
    return (into_image, into_text)


def local(picture_embeds, caption_embeds, positive_caption_ids, logit_multiplier, logit_shift):
    multiplier_scalar = logit_multiplier[0]
    shift_scalar = logit_shift[0]
    n_batch = lax.axis_size("batch")
    n_group = lax.axis_size("group")
    position = lax.axis_index("batch")
    member = lax.axis_index("group")
    pair_rows = caption_embeds.shape[0]
    own_unit32, own_inverse = unit_rows(picture_embeds)
    own_unit = own_unit32.astype(jnp.bfloat16)
    picture_unit_vectors, picture_class_ids = (
        lax.all_gather(own_unit, "group", axis=0, tiled=True),
        lax.all_gather(positive_caption_ids, "group", axis=0, tiled=True),
    )
    text_unit32, text_inverse = unit_rows(caption_embeds)
    caption_unit_vectors = text_unit32.astype(jnp.bfloat16)
    image_zero = jnp.zeros((picture_unit_vectors.shape[0], picture_embeds.shape[1]), jnp.float32)
    within = jnp.arange(pair_rows, dtype=jnp.int32)

    def cycle_turn(turn, state):
        similarity_tile, partial_value, image_sum = state
        source = jnp.mod(position - turn, n_batch)
        caption_count = (source * n_group + member) * pair_rows + within
        into_image, into_text = tile_loss_entries(
            picture_unit_vectors,
            picture_class_ids,
            similarity_tile,
            caption_count,
            multiplier_scalar,
            shift_scalar,
        )
        similarity_tile = shifted(similarity_tile, "batch", 1)
        partial_value = shifted(partial_value + into_text, "batch", 1)
        return (similarity_tile, partial_value, image_sum + into_image)

    start_state = (caption_unit_vectors, jnp.zeros(caption_embeds.shape, jnp.float32), image_zero)
    unused, text_up, image_up = lax.fori_loop(0, n_batch, cycle_turn, start_state)
    text_grad = (
        text_up - text_unit32 * jnp.sum(text_unit32 * text_up, axis=1, keepdims=True)
    ) * text_inverse
    own_up = lax.psum_scatter(image_up, "group", scatter_dimension=0, tiled=True)
    image_back = (
        own_up - own_unit32 * jnp.sum(own_unit32 * own_up, axis=1, keepdims=True)
    ) * own_inverse
    image_grad_t = lax.all_to_all(
        image_back.T.astype(jnp.bfloat16), "group", split_axis=0, concat_axis=1, tiled=True
    )
    return (image_grad_t, text_grad)


def solution(mesh):
    placed = (
        P(("batch", "group"), None),
        P(("batch", "group"), None),
        P(("batch", "group")),
        P(),
        P(),
    )
    return jax.shard_map(
        local,
        mesh=mesh,
        in_specs=placed,
        out_specs=(P("group", "batch"), P(("batch", "group"), None)),
        check_vma=False,
    )
```

profile of v0, /device:TPU:1, one launch (start us, length us, event | category | flops | bytes accessed | tf_op | source)
XLA Modules:
  0.0 407.6 jit_solution(8307424885772692868)
XLA Ops:
  12.8 10.8 %all-reduce = s32[1024]{0:T(1024)S(1)} all-reduce(s32[1024]{0:T(1024)S(1)} %dynamic-update-slice), channel_id=1, replica_groups=mesh['batch'=16,'group'=16] {'group'}, use_global_device_ids=true, to_apply=%add | all-reduce | flops 1024 | bytes 8192
  25.6 25.8 %all-gather.2.cloned.1.call-done = bf16[1024,1152]{1,0:T(8,128)(2,1)} async-done(((bf16[64,1152]{1,0:T(8,128)(2,1)}), bf16[1024,1152]{1,0:T(8,128)(2,1)}) %all-gather.2.cloned.1.call-update) | async-done | bytes 2359312 | tf_op jit(solution)/shard_map/all_gather | solution.py:62
  51.5 248.2 %while.20 = (s32[]{:T(128)}, bf16[64,1152]{1,0:T(8,128)(2,1)S(1)}, f32[64,1152]{1,0:T(8,128)S(1)}, f32[1024,1152]{1,0:T(8,128)}, f32[]{:T(128)}, /*index=5*/s32[...) while((s32[]{:T(128)}, bf16[64,1152]{1,0:T(8,128)(2,1)S(1)}, ...), condition=%wide.region_3.4_spmd.clone, body=%wide.region_2.3_spmd.clone.sunk | while | flops 456204352 | bytes 26940328 | solution.py:87
  63.0 7.2 %collective-permute-done.1 = f32[64,1152]{1,0:T(8,128)S(1)} collective-permute-done((f32[64,1152]{1,0:T(8,128)S(1)}, f32[64,1152]{1,0:T(8,128)S(1)}, u32[]{:S(2)}, u32[]{:S(2)}) %collective-permute-start.1) | collective-permute-done | bytes 294944 | tf_op jit(solution)/shard_map/while/body/eval_jaxpr/ppermute | solution.py:11
  77.5 5.3 %convolution_add_fusion.5 = f32[1024,1152]{1,0:T(8,128)} fusion(bf16[1024,64]{0,1:T(8,128)(2,1)S(1)} %fusion.45, bf16[64,1152]{1,0:T(8,128)(2,1)S(1)} %copy.19, f32[1024,1152]{1,0:T(8,128)} %get-tuple-element.404, pred[]{:T(512)S(6)} %compare.4), kind=kOutput, calls=%fused_computation.1.clone.1 | convolution fusion | flops 153354240 | bytes 9715713 | tf_op jit(solution)/shard_map/while/body/eval_jaxpr/dot_general | solution.py:41
  86.0 4.0 fusion.45
  92.0 5.3 %convolution_add_fusion.5 = f32[1024,1152]{1,0:T(8,128)} fusion(bf16[1024,64]{0,1:T(8,128)(2,1)S(1)} %fusion.45, bf16[64,1152]{1,0:T(8,128)(2,1)S(1)} %copy.19, f32[1024,1152]{1,0:T(8,128)} %get-tuple-element.404, pred[]{:T(512)S(6)} %compare.4), kind=kOutput, calls=%fused_computation.1.clone.1 | convolution fusion | flops 153354240 | bytes 9715713 | tf_op jit(solution)/shard_map/while/body/eval_jaxpr/dot_general | solution.py:41
  106.9 5.3 %convolution_add_fusion.5 = f32[1024,1152]{1,0:T(8,128)} fusion(bf16[1024,64]{0,1:T(8,128)(2,1)S(1)} %fusion.45, bf16[64,1152]{1,0:T(8,128)(2,1)S(1)} %copy.19, f32[1024,1152]{1,0:T(8,128)} %get-tuple-element.404, pred[]{:T(512)S(6)} %compare.4), kind=kOutput, calls=%fused_computation.1.clone.1 | convolution fusion | flops 153354240 | bytes 9715713 | tf_op jit(solution)/shard_map/while/body/eval_jaxpr/dot_general | solution.py:41
  121.4 5.3 %convolution_add_fusion.5 = f32[1024,1152]{1,0:T(8,128)} fusion(bf16[1024,64]{0,1:T(8,128)(2,1)S(1)} %fusion.45, bf16[64,1152]{1,0:T(8,128)(2,1)S(1)} %copy.19, f32[1024,1152]{1,0:T(8,128)} %get-tuple-element.404, pred[]{:T(512)S(6)} %compare.4), kind=kOutput, calls=%fused_computation.1.clone.1 | convolution fusion | flops 153354240 | bytes 9715713 | tf_op jit(solution)/shard_map/while/body/eval_jaxpr/dot_general | solution.py:41
  137.0 5.3 %convolution_add_fusion.5 = f32[1024,1152]{1,0:T(8,128)} fusion(bf16[1024,64]{0,1:T(8,128)(2,1)S(1)} %fusion.45, bf16[64,1152]{1,0:T(8,128)(2,1)S(1)} %copy.19, f32[1024,1152]{1,0:T(8,128)} %get-tuple-element.404, pred[]{:T(512)S(6)} %compare.4), kind=kOutput, calls=%fused_computation.1.clone.1 | convolution fusion | flops 153354240 | bytes 9715713 | tf_op jit(solution)/shard_map/while/body/eval_jaxpr/dot_general | solution.py:41
  152.2 5.3 %convolution_add_fusion.5 = f32[1024,1152]{1,0:T(8,128)} fusion(bf16[1024,64]{0,1:T(8,128)(2,1)S(1)} %fusion.45, bf16[64,1152]{1,0:T(8,128)(2,1)S(1)} %copy.19, f32[1024,1152]{1,0:T(8,128)} %get-tuple-element.404, pred[]{:T(512)S(6)} %compare.4), kind=kOutput, calls=%fused_computation.1.clone.1 | convolution fusion | flops 153354240 | bytes 9715713 | tf_op jit(solution)/shard_map/while/body/eval_jaxpr/dot_general | solution.py:41
  168.6 5.3 %convolution_add_fusion.5 = f32[1024,1152]{1,0:T(8,128)} fusion(bf16[1024,64]{0,1:T(8,128)(2,1)S(1)} %fusion.45, bf16[64,1152]{1,0:T(8,128)(2,1)S(1)} %copy.19, f32[1024,1152]{1,0:T(8,128)} %get-tuple-element.404, pred[]{:T(512)S(6)} %compare.4), kind=kOutput, calls=%fused_computation.1.clone.1 | convolution fusion | flops 153354240 | bytes 9715713 | tf_op jit(solution)/shard_map/while/body/eval_jaxpr/dot_general | solution.py:41
  176.7 4.0 fusion.45
  183.8 5.3 %convolution_add_fusion.5 = f32[1024,1152]{1,0:T(8,128)} fusion(bf16[1024,64]{0,1:T(8,128)(2,1)S(1)} %fusion.45, bf16[64,1152]{1,0:T(8,128)(2,1)S(1)} %copy.19, f32[1024,1152]{1,0:T(8,128)} %get-tuple-element.404, pred[]{:T(512)S(6)} %compare.4), kind=kOutput, calls=%fused_computation.1.clone.1 | convolution fusion | flops 153354240 | bytes 9715713 | tf_op jit(solution)/shard_map/while/body/eval_jaxpr/dot_general | solution.py:41
  200.1 5.3 %convolution_add_fusion.5 = f32[1024,1152]{1,0:T(8,128)} fusion(bf16[1024,64]{0,1:T(8,128)(2,1)S(1)} %fusion.45, bf16[64,1152]{1,0:T(8,128)(2,1)S(1)} %copy.19, f32[1024,1152]{1,0:T(8,128)} %get-tuple-element.404, pred[]{:T(512)S(6)} %compare.4), kind=kOutput, calls=%fused_computation.1.clone.1 | convolution fusion | flops 153354240 | bytes 9715713 | tf_op jit(solution)/shard_map/while/body/eval_jaxpr/dot_general | solution.py:41
  215.0 5.3 %convolution_add_fusion.5 = f32[1024,1152]{1,0:T(8,128)} fusion(bf16[1024,64]{0,1:T(8,128)(2,1)S(1)} %fusion.45, bf16[64,1152]{1,0:T(8,128)(2,1)S(1)} %copy.19, f32[1024,1152]{1,0:T(8,128)} %get-tuple-element.404, pred[]{:T(512)S(6)} %compare.4), kind=kOutput, calls=%fused_computation.1.clone.1 | convolution fusion | flops 153354240 | bytes 9715713 | tf_op jit(solution)/shard_map/while/body/eval_jaxpr/dot_general | solution.py:41
  230.8 5.3 %convolution_add_fusion.5 = f32[1024,1152]{1,0:T(8,128)} fusion(bf16[1024,64]{0,1:T(8,128)(2,1)S(1)} %fusion.45, bf16[64,1152]{1,0:T(8,128)(2,1)S(1)} %copy.19, f32[1024,1152]{1,0:T(8,128)} %get-tuple-element.404, pred[]{:T(512)S(6)} %compare.4), kind=kOutput, calls=%fused_computation.1.clone.1 | convolution fusion | flops 153354240 | bytes 9715713 | tf_op jit(solution)/shard_map/while/body/eval_jaxpr/dot_general | solution.py:41
  245.6 5.3 %convolution_add_fusion.5 = f32[1024,1152]{1,0:T(8,128)} fusion(bf16[1024,64]{0,1:T(8,128)(2,1)S(1)} %fusion.45, bf16[64,1152]{1,0:T(8,128)(2,1)S(1)} %copy.19, f32[1024,1152]{1,0:T(8,128)} %get-tuple-element.404, pred[]{:T(512)S(6)} %compare.4), kind=kOutput, calls=%fused_computation.1.clone.1 | convolution fusion | flops 153354240 | bytes 9715713 | tf_op jit(solution)/shard_map/while/body/eval_jaxpr/dot_general | solution.py:41
  261.0 5.3 %convolution_add_fusion.5 = f32[1024,1152]{1,0:T(8,128)} fusion(bf16[1024,64]{0,1:T(8,128)(2,1)S(1)} %fusion.45, bf16[64,1152]{1,0:T(8,128)(2,1)S(1)} %copy.19, f32[1024,1152]{1,0:T(8,128)} %get-tuple-element.404, pred[]{:T(512)S(6)} %compare.4), kind=kOutput, calls=%fused_computation.1.clone.1 | convolution fusion | flops 153354240 | bytes 9715713 | tf_op jit(solution)/shard_map/while/body/eval_jaxpr/dot_general | solution.py:41
  274.5 5.3 %convolution_add_fusion.5 = f32[1024,1152]{1,0:T(8,128)} fusion(bf16[1024,64]{0,1:T(8,128)(2,1)S(1)} %fusion.45, bf16[64,1152]{1,0:T(8,128)(2,1)S(1)} %copy.19, f32[1024,1152]{1,0:T(8,128)} %get-tuple-element.404, pred[]{:T(512)S(6)} %compare.4), kind=kOutput, calls=%fused_computation.1.clone.1 | convolution fusion | flops 153354240 | bytes 9715713 | tf_op jit(solution)/shard_map/while/body/eval_jaxpr/dot_general | solution.py:41
  291.4 5.3 %convolution_add_fusion.5 = f32[1024,1152]{1,0:T(8,128)} fusion(bf16[1024,64]{0,1:T(8,128)(2,1)S(1)} %fusion.45, bf16[64,1152]{1,0:T(8,128)(2,1)S(1)} %copy.19, f32[1024,1152]{1,0:T(8,128)} %get-tuple-element.404, pred[]{:T(512)S(6)} %compare.4), kind=kOutput, calls=%fused_computation.1.clone.1 | convolution fusion | flops 153354240 | bytes 9715713 | tf_op jit(solution)/shard_map/while/body/eval_jaxpr/dot_general | solution.py:41
  300.8 80.8 %reduce-scatter.2.cloned.1.call-done = f32[64,1152]{1,0:T(8,128)} async-done(((f32[1024,1152]{1,0:T(8,128)}), f32[64,1152]{1,0:T(8,128)}) %reduce-scatter.2.cloned.1.call-update) | async-done | bytes 294928 | tf_op jit(solution)/shard_map/reduce_scatter | solution.py:91
  385.2 7.5 %all-to-all-start = ((bf16[16,72,64]{1,2,0:T(8,128)(2,1)}), bf16[16,72,64]{1,2,0:T(8,128)(2,1)S(1)}, u32[]{:S(2)}, u32[]{:S(2)}) async-start(bf16[16,72,64]{1,2,0:T(8,128)(2,1)} %copy.10), calls=%async_computation.1 | async-start | bytes 524288 | tf_op jit(solution)/shard_map/all_to_all | solution.py:95
  393.5 6.4 %all-to-all-done = bf16[16,72,64]{1,2,0:T(8,128)(2,1)S(1)} async-done(((bf16[16,72,64]{1,2,0:T(8,128)(2,1)}), bf16[16,72,64]{1,2,0:T(8,128)(2,1)S(1)}, u32[]{:S(2)}, u32[]{:S(2)}) %all-to-all-start) | async-done | bytes 147488 | tf_op jit(solution)/shard_map/all_to_all | solution.py:95
  (184 shorter events, 166.4 us)
Async XLA Ops:
  7.2 44.3 %all-gather.2.cloned.1.call-start = ((), (), s32[]{:S(2)}) async-start(), calls=%async_computation.2 | async-start | bytes 2506752 | tf_op jit(solution)/shard_map/all_gather | solution.py:62
  10.0 371.7 %reduce-scatter.2.cloned.1.call-start = ((), (), s32[]{:S(2)}) async-start(), calls=%async_computation.3 | async-start | bytes 5013504 | tf_op jit(solution)/shard_map/reduce_scatter | solution.py:91
  51.5 11.5 %collective-permute-start = (bf16[64,1152]{1,0:T(8,128)(2,1)S(1)}, bf16[64,1152]{1,0:T(8,128)(2,1)S(1)}, u32[]{:S(2)}, u32[]{:S(2)}) collective-permute-start(bf16[64,1152]{1,0:T(8,128)(2,1)S(1)} %copy.19), channel_id=1, source_target_pairs={{0,16},{16,32},{32,48},{48,64},{64,80},{80,96},{96,112},{112,128},... | collective-permute-start | bytes 442376 | tf_op jit(solution)/shard_map/while/body/eval_jaxpr/ppermute | solution.py:11
  58.5 11.7 %collective-permute-start.1 = (f32[64,1152]{1,0:T(8,128)S(1)}, f32[64,1152]{1,0:T(8,128)S(1)}, u32[]{:S(2)}, u32[]{:S(2)}) collective-permute-start(f32[64,1152]{1,0:T(8,128)S(1)} %convolution_add_fusion.4), channel_id=1, source_target_pairs={{0,16},{16,32},{32,48},{48,64},{64,80},{80,96},{96,112},{112,128},... | collective-permute-start | bytes 884744 | tf_op jit(solution)/shard_map/while/body/eval_jaxpr/ppermute | solution.py:11
  70.2 12.6 %collective-permute-start = (bf16[64,1152]{1,0:T(8,128)(2,1)S(1)}, bf16[64,1152]{1,0:T(8,128)(2,1)S(1)}, u32[]{:S(2)}, u32[]{:S(2)}) collective-permute-start(bf16[64,1152]{1,0:T(8,128)(2,1)S(1)} %copy.19), channel_id=1, source_target_pairs={{0,16},{16,32},{32,48},{48,64},{64,80},{80,96},{96,112},{112,128},... | collective-permute-start | bytes 442376 | tf_op jit(solution)/shard_map/while/body/eval_jaxpr/ppermute | solution.py:11
  74.9 10.8 %collective-permute-start.1 = (f32[64,1152]{1,0:T(8,128)S(1)}, f32[64,1152]{1,0:T(8,128)S(1)}, u32[]{:S(2)}, u32[]{:S(2)}) collective-permute-start(f32[64,1152]{1,0:T(8,128)S(1)} %convolution_add_fusion.4), channel_id=1, source_target_pairs={{0,16},{16,32},{32,48},{48,64},{64,80},{80,96},{96,112},{112,128},... | collective-permute-start | bytes 884744 | tf_op jit(solution)/shard_map/while/body/eval_jaxpr/ppermute | solution.py:11
  85.6 11.6 %collective-permute-start = (bf16[64,1152]{1,0:T(8,128)(2,1)S(1)}, bf16[64,1152]{1,0:T(8,128)(2,1)S(1)}, u32[]{:S(2)}, u32[]{:S(2)}) collective-permute-start(bf16[64,1152]{1,0:T(8,128)(2,1)S(1)} %copy.19), channel_id=1, source_target_pairs={{0,16},{16,32},{32,48},{48,64},{64,80},{80,96},{96,112},{112,128},... | collective-permute-start | bytes 442376 | tf_op jit(solution)/shard_map/while/body/eval_jaxpr/ppermute | solution.py:11
  99.8 12.4 %collective-permute-start = (bf16[64,1152]{1,0:T(8,128)(2,1)S(1)}, bf16[64,1152]{1,0:T(8,128)(2,1)S(1)}, u32[]{:S(2)}, u32[]{:S(2)}) collective-permute-start(bf16[64,1152]{1,0:T(8,128)(2,1)S(1)} %copy.19), channel_id=1, source_target_pairs={{0,16},{16,32},{32,48},{48,64},{64,80},{80,96},{96,112},{112,128},... | collective-permute-start | bytes 442376 | tf_op jit(solution)/shard_map/while/body/eval_jaxpr/ppermute | solution.py:11
  104.5 10.8 %collective-permute-start.1 = (f32[64,1152]{1,0:T(8,128)S(1)}, f32[64,1152]{1,0:T(8,128)S(1)}, u32[]{:S(2)}, u32[]{:S(2)}) collective-permute-start(f32[64,1152]{1,0:T(8,128)S(1)} %convolution_add_fusion.4), channel_id=1, source_target_pairs={{0,16},{16,32},{32,48},{48,64},{64,80},{80,96},{96,112},{112,128},... | collective-permute-start | bytes 884744 | tf_op jit(solution)/shard_map/while/body/eval_jaxpr/ppermute | solution.py:11
  115.3 11.3 %collective-permute-start = (bf16[64,1152]{1,0:T(8,128)(2,1)S(1)}, bf16[64,1152]{1,0:T(8,128)(2,1)S(1)}, u32[]{:S(2)}, u32[]{:S(2)}) collective-permute-start(bf16[64,1152]{1,0:T(8,128)(2,1)S(1)} %copy.19), channel_id=1, source_target_pairs={{0,16},{16,32},{32,48},{48,64},{64,80},{80,96},{96,112},{112,128},... | collective-permute-start | bytes 442376 | tf_op jit(solution)/shard_map/while/body/eval_jaxpr/ppermute | solution.py:11
  130.2 12.1 %collective-permute-start = (bf16[64,1152]{1,0:T(8,128)(2,1)S(1)}, bf16[64,1152]{1,0:T(8,128)(2,1)S(1)}, u32[]{:S(2)}, u32[]{:S(2)}) collective-permute-start(bf16[64,1152]{1,0:T(8,128)(2,1)S(1)} %copy.19), channel_id=1, source_target_pairs={{0,16},{16,32},{32,48},{48,64},{64,80},{80,96},{96,112},{112,128},... | collective-permute-start | bytes 442376 | tf_op jit(solution)/shard_map/while/body/eval_jaxpr/ppermute | solution.py:11
  134.8 10.8 %collective-permute-start.1 = (f32[64,1152]{1,0:T(8,128)S(1)}, f32[64,1152]{1,0:T(8,128)S(1)}, u32[]{:S(2)}, u32[]{:S(2)}) collective-permute-start(f32[64,1152]{1,0:T(8,128)S(1)} %convolution_add_fusion.4), channel_id=1, source_target_pairs={{0,16},{16,32},{32,48},{48,64},{64,80},{80,96},{96,112},{112,128},... | collective-permute-start | bytes 884744 | tf_op jit(solution)/shard_map/while/body/eval_jaxpr/ppermute | solution.py:11
  145.7 11.8 %collective-permute-start = (bf16[64,1152]{1,0:T(8,128)(2,1)S(1)}, bf16[64,1152]{1,0:T(8,128)(2,1)S(1)}, u32[]{:S(2)}, u32[]{:S(2)}) collective-permute-start(bf16[64,1152]{1,0:T(8,128)(2,1)S(1)} %copy.19), channel_id=1, source_target_pairs={{0,16},{16,32},{32,48},{48,64},{64,80},{80,96},{96,112},{112,128},... | collective-permute-start | bytes 442376 | tf_op jit(solution)/shard_map/while/body/eval_jaxpr/ppermute | solution.py:11
  161.1 12.8 %collective-permute-start = (bf16[64,1152]{1,0:T(8,128)(2,1)S(1)}, bf16[64,1152]{1,0:T(8,128)(2,1)S(1)}, u32[]{:S(2)}, u32[]{:S(2)}) collective-permute-start(bf16[64,1152]{1,0:T(8,128)(2,1)S(1)} %copy.19), channel_id=1, source_target_pairs={{0,16},{16,32},{32,48},{48,64},{64,80},{80,96},{96,112},{112,128},... | collective-permute-start | bytes 442376 | tf_op jit(solution)/shard_map/while/body/eval_jaxpr/ppermute | solution.py:11
  176.3 12.8 %collective-permute-start = (bf16[64,1152]{1,0:T(8,128)(2,1)S(1)}, bf16[64,1152]{1,0:T(8,128)(2,1)S(1)}, u32[]{:S(2)}, u32[]{:S(2)}) collective-permute-start(bf16[64,1152]{1,0:T(8,128)(2,1)S(1)} %copy.19), channel_id=1, source_target_pairs={{0,16},{16,32},{32,48},{48,64},{64,80},{80,96},{96,112},{112,128},... | collective-permute-start | bytes 442376 | tf_op jit(solution)/shard_map/while/body/eval_jaxpr/ppermute | solution.py:11
  190.6 14.8 %collective-permute-start = (bf16[64,1152]{1,0:T(8,128)(2,1)S(1)}, bf16[64,1152]{1,0:T(8,128)(2,1)S(1)}, u32[]{:S(2)}, u32[]{:S(2)}) collective-permute-start(bf16[64,1152]{1,0:T(8,128)(2,1)S(1)} %copy.19), channel_id=1, source_target_pairs={{0,16},{16,32},{32,48},{48,64},{64,80},{80,96},{96,112},{112,128},... | collective-permute-start | bytes 442376 | tf_op jit(solution)/shard_map/while/body/eval_jaxpr/ppermute | solution.py:11
  206.2 14.0 %collective-permute-start = (bf16[64,1152]{1,0:T(8,128)(2,1)S(1)}, bf16[64,1152]{1,0:T(8,128)(2,1)S(1)}, u32[]{:S(2)}, u32[]{:S(2)}) collective-permute-start(bf16[64,1152]{1,0:T(8,128)(2,1)S(1)} %copy.19), channel_id=1, source_target_pairs={{0,16},{16,32},{32,48},{48,64},{64,80},{80,96},{96,112},{112,128},... | collective-permute-start | bytes 442376 | tf_op jit(solution)/shard_map/while/body/eval_jaxpr/ppermute | solution.py:11
  221.5 14.5 %collective-permute-start = (bf16[64,1152]{1,0:T(8,128)(2,1)S(1)}, bf16[64,1152]{1,0:T(8,128)(2,1)S(1)}, u32[]{:S(2)}, u32[]{:S(2)}) collective-permute-start(bf16[64,1152]{1,0:T(8,128)(2,1)S(1)} %copy.19), channel_id=1, source_target_pairs={{0,16},{16,32},{32,48},{48,64},{64,80},{80,96},{96,112},{112,128},... | collective-permute-start | bytes 442376 | tf_op jit(solution)/shard_map/while/body/eval_jaxpr/ppermute | solution.py:11
  237.3 13.6 %collective-permute-start = (bf16[64,1152]{1,0:T(8,128)(2,1)S(1)}, bf16[64,1152]{1,0:T(8,128)(2,1)S(1)}, u32[]{:S(2)}, u32[]{:S(2)}) collective-permute-start(bf16[64,1152]{1,0:T(8,128)(2,1)S(1)} %copy.19), channel_id=1, source_target_pairs={{0,16},{16,32},{32,48},{48,64},{64,80},{80,96},{96,112},{112,128},... | collective-permute-start | bytes 442376 | tf_op jit(solution)/shard_map/while/body/eval_jaxpr/ppermute | solution.py:11
  252.1 14.2 %collective-permute-start = (bf16[64,1152]{1,0:T(8,128)(2,1)S(1)}, bf16[64,1152]{1,0:T(8,128)(2,1)S(1)}, u32[]{:S(2)}, u32[]{:S(2)}) collective-permute-start(bf16[64,1152]{1,0:T(8,128)(2,1)S(1)} %copy.19), channel_id=1, source_target_pairs={{0,16},{16,32},{32,48},{48,64},{64,80},{80,96},{96,112},{112,128},... | collective-permute-start | bytes 442376 | tf_op jit(solution)/shard_map/while/body/eval_jaxpr/ppermute | solution.py:11
  267.5 12.3 %collective-permute-start = (bf16[64,1152]{1,0:T(8,128)(2,1)S(1)}, bf16[64,1152]{1,0:T(8,128)(2,1)S(1)}, u32[]{:S(2)}, u32[]{:S(2)}) collective-permute-start(bf16[64,1152]{1,0:T(8,128)(2,1)S(1)} %copy.19), channel_id=1, source_target_pairs={{0,16},{16,32},{32,48},{48,64},{64,80},{80,96},{96,112},{112,128},... | collective-permute-start | bytes 442376 | tf_op jit(solution)/shard_map/while/body/eval_jaxpr/ppermute | solution.py:11
  282.3 14.4 %collective-permute-start = (bf16[64,1152]{1,0:T(8,128)(2,1)S(1)}, bf16[64,1152]{1,0:T(8,128)(2,1)S(1)}, u32[]{:S(2)}, u32[]{:S(2)}) collective-permute-start(bf16[64,1152]{1,0:T(8,128)(2,1)S(1)} %copy.19), channel_id=1, source_target_pairs={{0,16},{16,32},{32,48},{48,64},{64,80},{80,96},{96,112},{112,128},... | collective-permute-start | bytes 442376 | tf_op jit(solution)/shard_map/while/body/eval_jaxpr/ppermute | solution.py:11
  288.1 11.6 %collective-permute-start.1 = (f32[64,1152]{1,0:T(8,128)S(1)}, f32[64,1152]{1,0:T(8,128)S(1)}, u32[]{:S(2)}, u32[]{:S(2)}) collective-permute-start(f32[64,1152]{1,0:T(8,128)S(1)} %convolution_add_fusion.4), channel_id=1, source_target_pairs={{0,16},{16,32},{32,48},{48,64},{64,80},{80,96},{96,112},{112,128},... | collective-permute-start | bytes 884744 | tf_op jit(solution)/shard_map/while/body/eval_jaxpr/ppermute | solution.py:11
  385.2 14.8 %all-to-all-start = ((bf16[16,72,64]{1,2,0:T(8,128)(2,1)}), bf16[16,72,64]{1,2,0:T(8,128)(2,1)S(1)}, u32[]{:S(2)}, u32[]{:S(2)}) async-start(bf16[16,72,64]{1,2,0:T(8,128)(2,1)} %copy.10), calls=%async_computation.1 | async-start | bytes 524288 | tf_op jit(solution)/shard_map/all_to_all | solution.py:95
  (29 other events, 266.6 us)
Sparse Core Ops, SparseCore 0:
  10.4 41.0 all-gather.1
  299.8 81.7 reduce-scatter.1
where the time goes:
time: 409 us; the launch traced here: 408 us
  waiting for transfers between devices  154 us (38%)
  matrix products  153 us (37%)
  starting transfers between devices  60.6 us (15%)
  between operations  14.7 us (4%)
  blocking collectives  10.8 us (3%)
  other arithmetic  8.12 us (2%)
  local copies, waits for them, and re-layouts  5.31 us (1%)
    dot_general x16, matrix products, tile_loss_entries(): jnp.dot(entry_factor, caption_slice, preferred_element_type=jnp.float32)  82 us
    reduce_scatter x1, waiting for transfers between devices, local(): lax.psum_scatter(image_up, 'group', scatter_dimension=0, tiled=True)  80.8 us
    dot_general x16, matrix products, tile_loss_entries(): lax.dot_general(picture_unit_vectors, caption_slice, (((1,), (1,)), ((),...  62.5 us
    ppermute x32, starting transfers between devices, shifted(): lax.ppermute(shard, axis, [(i, (i + by) % size) for i in range(size)])  52.9 us
    ppermute x32, waiting for transfers between devices, shifted(): lax.ppermute(shard, axis, [(i, (i + by) % size) for i in range(size)])  41.2 us
    all_gather x1, waiting for transfers between devices, local(): lax.all_gather(own_unit, 'group', axis=0, tiled=True)  25.8 us
    unnamed x1, blocking collectives  10.8 us
    dot_general x16, matrix products, tile_loss_entries(): lax.dot_general(entry_factor, picture_unit_vectors, (((0,), (0,)), ((), (...  8.51 us
  transfers between devices with their start and end apart: 35, of which 19 were waited for; matrix products, arithmetic and copies ran while one was open for 39% of the time, Pallas kernels for 0%

commit v1 on v0

v1 whole, which is shorter than its diff:
```python
import functools

import jax
import jax.numpy as jnp
from jax import lax
from jax.experimental import pallas as pl
from jax.experimental.pallas import tpu as pltpu
from jax.sharding import PartitionSpec as P

EPS = 1e-06
ROWS = 64
HALF = ROWS // 2
D = 1152
SIDE = 4
NZ = 8
FEAT = D // 8
PART = D // 16
LOG2E = 1.4426950408889634
f32 = jnp.float32
bf16 = jnp.bfloat16


def rdma(src, dst, ssem, rsem, dev):
    return pltpu.make_async_remote_copy(
        src_ref=src, dst_ref=dst, send_sem=ssem, recv_sem=rsem,
        device_id=dev, device_id_type=pl.DeviceIdType.MESH)


def unit_rows(values):
    wide = values.astype(f32)
    inverse = lax.rsqrt(jnp.sum(wide * wide, axis=1, keepdims=True) + EPS)
    return wide * inverse, inverse


def kernel(pic, cap, lab, mul, shift, img_out, txt_out,
           U, M, T, Ut, Tt, W, tacc, svec, own, sib_out, sib_in,
           tstage, trecv, G, rbh, rbf, rah, raf, r1, fin, fin_in,
           us, ur, ms, mr, zs, zr, bs, br, ts, tr, gs, gr, xs, xr):
    batch = lax.axis_index("batch")
    group = lax.axis_index("group")
    z, yh = batch // 2, batch % 2
    core = group % 2
    x = (group // 2) % SIDE
    y = yh * 2 + group // (2 * SIDE)
    m = mul[0]
    b = shift[0]

    def dev(x_, y_, z_, c_):
        return (z_ * 2 + y_ // 2, ((y_ % 2) * SIDE + x_) * 2 + c_)

    first = core == 0
    pa = jnp.where(first, x, y)
    pb = jnp.where(first, y, x)

    def slot(ka, kb):
        a_ = (pa + ka) % SIDE
        b_ = (pb + kb) % SIDE
        return jnp.where(first, b_ * SIDE + a_, a_ * SIDE + b_)

    def plane(ka, kb):
        a_ = (pa + ka) % SIDE
        b_ = (pb + kb) % SIDE
        return dev(jnp.where(first, a_, b_), jnp.where(first, b_, a_), z, core)

    a_dev = (plane(1, 0), plane(SIDE - 1, 0))
    b_dev = (plane(0, 1), plane(0, SIDE - 1))
    z_dev = (dev(x, y, (z + 1) % NZ, core), dev(x, y, (z + NZ - 1) % NZ, core))
    sib = dev(x, y, z, 1 - core)

    barrier = pltpu.get_barrier_semaphore()
    for d in (*a_dev, *b_dev, *z_dev, sib):
        pl.semaphore_signal(barrier, inc=1, device_id=d, device_id_type=pl.DeviceIdType.MESH)

    me = slot(0, 0)
    p_unit, p_inv = unit_rows(pic[...])
    U[me] = p_unit.astype(bf16).reshape(2, HALF, D)
    t_unit, t_inv = unit_rows(cap[...])
    T[0] = t_unit.astype(bf16).reshape(2, HALF, D)
    spread = jnp.broadcast_to(p_inv, (ROWS, 128))
    inv_lane = jnp.concatenate([spread, spread], axis=0).T[0:8]
    lab_row = lab[...].astype(f32)
    lab_lane = jnp.broadcast_to(jnp.concatenate([lab_row, lab_row], axis=1), (8, 128))
    row8 = lax.broadcasted_iota(jnp.int32, (8, 128), 0)
    lane8 = lax.broadcasted_iota(jnp.int32, (8, 128), 1)
    meta = jnp.where(row8 == 0, inv_lane, jnp.where(row8 == 1, lab_lane, 0.0))
    M[me] = jnp.where(lane8 // ROWS == x % 2, meta, 0.0)

    pl.semaphore_wait(barrier, 7)

    started = []

    def go(copy):
        copy.start()
        started.append(copy)

    def img_full(i, j, slot_, dst):
        go(rdma(U.at[slot_], U.at[slot_], us.at[i], ur.at[i], dst))
        go(rdma(M.at[slot_], M.at[slot_], ms.at[j], mr.at[j], dst))

    def img_half(i, slot_, hf, dst):
        go(rdma(U.at[slot_, hf], U.at[slot_, hf], us.at[i], ur.at[i], dst))

    def meta_only(j, slot_, dst):
        go(rdma(M.at[slot_], M.at[slot_], ms.at[j], mr.at[j], dst))

    def got_img(i, slot_):
        rdma(U.at[slot_], U.at[slot_], us.at[i], ur.at[i], sib).wait_recv()

    def got_half(i, slot_, hf):
        rdma(U.at[slot_, hf], U.at[slot_, hf], us.at[i], ur.at[i], sib).wait_recv()

    def got_meta(j, slot_):
        rdma(M.at[slot_], M.at[slot_], ms.at[j], mr.at[j], sib).wait_recv()

    def b1(ka):
        img_full(4 + 2 * ka, 3 + 2 * ka, slot(ka, 0), b_dev[0])
        img_full(5 + 2 * ka, 4 + 2 * ka, slot(ka, 0), b_dev[1])

    def b2(ka):
        before, after = slot(ka, SIDE - 1), slot(ka, 1)
        got_img(4 + 2 * ka, before)
        img_half(12 + 2 * ka, before, 0, b_dev[0])
        got_meta(3 + 2 * ka, before)
        meta_only(11 + ka, before, b_dev[0])
        got_img(5 + 2 * ka, after)
        img_half(13 + 2 * ka, after, 1, b_dev[1])
        got_meta(4 + 2 * ka, after)

    def b3(ka):
        far = slot(ka, 2)
        got_half(12 + 2 * ka, far, 0)
        got_half(13 + 2 * ka, far, 1)
        got_meta(11 + ka, far)

    def to_sib(k):
        go(rdma(T.at[k], T.at[NZ + k], bs.at[k], br.at[k], sib))

    def z_send(i, k, d):
        to = (k + NZ - 1) % NZ if d == 0 else (k + 1) % NZ
        go(rdma(T.at[k], T.at[to], zs.at[i], zr.at[i], z_dev[d]))

    def z_got(i, k):
        rdma(T.at[k], T.at[k], zs.at[i], zr.at[i], sib).wait_recv()

    z_send(0, 0, 0)
    z_send(1, 0, 1)
    img_full(0, 0, me, a_dev[0])
    img_full(1, 1, me, a_dev[1])
    b1(0)
    to_sib(0)
    before, after = slot(SIDE - 1, 0), slot(1, 0)
    got_img(0, before)
    img_half(2, before, 0, a_dev[0])
    got_meta(0, before)
    meta_only(2, before, a_dev[0])
    b1(3)
    got_img(1, after)
    img_half(3, after, 1, a_dev[1])
    got_meta(1, after)
    b1(1)
    z_got(0, 7)
    z_send(2, 7, 0)
    to_sib(7)
    z_got(1, 1)
    z_send(3, 1, 1)
    to_sib(1)
    b2(0)
    far = slot(2, 0)
    got_half(2, far, 0)
    got_half(3, far, 1)
    got_meta(2, far)
    b1(2)
    z_got(2, 6)
    z_send(4, 6, 0)
    to_sib(6)
    z_got(3, 2)
    z_send(5, 2, 1)
    to_sib(2)
    b2(3)
    b2(1)
    z_got(4, 5)
    go(rdma(T.at[5, 0], T.at[4, 0], zs.at[6], zr.at[6], z_dev[0]))
    to_sib(5)
    z_got(5, 3)
    go(rdma(T.at[3, 1], T.at[4, 1], zs.at[7], zr.at[7], z_dev[1]))
    to_sib(3)
    b2(2)
    for ka in (0, 3, 1, 2):
        b3(ka)
    rdma(T.at[4, 0], T.at[4, 0], zs.at[6], zr.at[6], sib).wait_recv()
    rdma(T.at[4, 1], T.at[4, 1], zs.at[7], zr.at[7], sib).wait_recv()
    to_sib(4)
    for k in (0, 7, 1, 6, 2, 5, 3, 4):
        rdma(T.at[NZ + k], T.at[NZ + k], bs.at[k], br.at[k], sib).wait_recv()

    @pl.loop(0, 4)
    def _(q):
        Ut[q] = U[pl.ds(q * 4, 4)].reshape(4 * ROWS, D).T

    for q in range(4):
        Tt[:, q * 256:(q + 1) * 256] = T[4 * q:4 * q + 4].reshape(4 * ROWS, D).T

    base = yh * 1024 + (group // 2) * 128
    k1 = m * LOG2E
    k2 = b * LOG2E

    def lane_vec(q, r):
        lo = M[q * 4, r:r + 1] + M[q * 4 + 1, r:r + 1]
        hi = M[q * 4 + 2, r:r + 1] + M[q * 4 + 3, r:r + 1]
        return jnp.concatenate([lo, hi], axis=1)

    tacc[...] = jnp.zeros_like(tacc)
    svec[...] = jnp.zeros_like(svec)

    @pl.loop(0, 8)
    def _(step):
        q = step // 2
        hf = step % 2
        rows = T[pl.ds(hf * NZ, NZ)].reshape(512, D)
        images = U[pl.ds(q * 4, 4)].reshape(256, D)
        cos = lax.dot_general(rows, images, (((1,), (1,)), ((), ())), preferred_element_type=f32)
        r = lax.broadcasted_iota(jnp.int32, (512, 1), 0)
        owner = jnp.where(hf == 0, core, 1 - core)
        ids = ((z + (r >> 6)) & 7) * 2048 + (base + owner * ROWS) + (r & 63)
        match = ids.astype(f32) == lane_vec(q, 1)
        logit = cos * k1 + k2
        e = jnp.exp2(jnp.where(match, logit, -logit))
        w = (jnp.where(match, -m, m) / (1.0 + e)).astype(bf16)
        at = pl.multiple_of(q * 256, 256)
        W[pl.ds(pl.multiple_of(hf * 512, 512), 512), pl.ds(at, 256)] = w
        wc = w.astype(f32) * cos
        svec[q] += jnp.broadcast_to(jnp.sum(wc, axis=0, keepdims=True), (8, 256))
        tacc[hf] += wc[:, :128] + wc[:, 128:]

    images = U[...].reshape(1024, D)

    def text_part(hf, lo, n):
        up = jnp.dot(W[hf * 512:hf * 512 + 512, :], images[:, lo:lo + n], preferred_element_type=f32)
        along = jnp.sum(tacc[hf], axis=1, keepdims=True)
        return up - T[hf * NZ:hf * NZ + NZ, :, :, lo:lo + n].reshape(512, n).astype(f32) * along

    cuts = [(0, 256), (256, 256), (512, 256), (768, 256), (1024, 128)]
    for lo, n in cuts:
        sib_out[:, :, :, lo:lo + n] = text_part(1, lo, n).astype(bf16).reshape(NZ, 2, HALF, n)
    swap = rdma(sib_out, sib_in, xs.at[0], xr.at[0], sib)
    go(swap)
    for lo, n in cuts:
        own[:, :, :, lo:lo + n] = text_part(0, lo, n).reshape(NZ, 2, HALF, n)

    @pl.loop(0, 4)
    def _(q):
        at = pl.multiple_of(q * 256, 256)
        up = jnp.dot(Tt[...], W[:, pl.ds(at, 256)], preferred_element_type=f32)
        along = svec[q][0:1]
        inv = lane_vec(q, 0)
        for g in range(8):
            lo = g * FEAT
            part = (up[lo:lo + FEAT] - Ut[q, lo:lo + FEAT].astype(f32) * along) * inv
            G[(q // 2) * 8 + g, q % 2] = part.astype(bf16)

    def text_sum(k):
        return own[k] + sib_in[k].astype(f32)

    def t_copy(d, i):
        src, dst = tstage.at[d, i], trecv.at[d, i]
        if i == 0:
            src, dst = tstage.at[d, 0, d], trecv.at[d, 0, d]
        return rdma(src, dst, ts.at[4 * d + i], tr.at[4 * d + i], z_dev[d])

    def t_step(i):
        for d in (0, 1):
            k = 4 - i if d == 0 else 4 + i
            if i == 0:
                tstage[d, 0, d] = (own[4, d] + sib_in[4, d].astype(f32)).astype(bf16)
            else:
                t_copy(d, i - 1).wait_recv()
                if i == 1:
                    tstage[d, 1, d] = (own[k, d] + sib_in[k, d].astype(f32)
                                       + trecv[d, 0, d].astype(f32)).astype(bf16)
                    tstage[d, 1, 1 - d] = (own[k, 1 - d] + sib_in[k, 1 - d].astype(f32)).astype(bf16)
                else:
                    tstage[d, i] = (text_sum(k) + trecv[d, i - 1].astype(f32)).astype(bf16)
            go(t_copy(d, i))

    def gb_first(ka):
        for d in (0, 1):
            go(rdma(G.at[slot(ka, 2), d], rbh.at[ka, d], gs.at[2 * ka + d], gr.at[2 * ka + d], b_dev[d]))

    def gb_second(ka):
        for d in (0, 1):
            at = slot(ka, 1 if d == 0 else SIDE - 1)
            rdma(rbh.at[ka, d], rbh.at[ka, d], gs.at[2 * ka + d], gr.at[2 * ka + d], sib).wait_recv()
            G[at, d] = (G[at, d].astype(f32) + rbh[ka, d].astype(f32)).astype(bf16)
            go(rdma(G.at[at], rbf.at[ka, d], gs.at[8 + 2 * ka + d], gr.at[8 + 2 * ka + d], b_dev[d]))

    def gb_last(ka):
        for d in (0, 1):
            i = 8 + 2 * ka + d
            rdma(rbf.at[ka, d], rbf.at[ka, d], gs.at[i], gr.at[i], sib).wait_recv()
        return G[slot(ka, 0)].astype(f32) + rbf[ka, 0].astype(f32) + rbf[ka, 1].astype(f32)

    order = (2, 1, 3, 0)
    for ka in order:
        gb_first(ka)
    swap.wait_recv()
    t_step(0)
    for ka in order:
        gb_second(ka)
    t_step(1)
    r1[0] = gb_last(2).astype(bf16)
    for d in (0, 1):
        go(rdma(r1.at[0, d], rah.at[d], gs.at[16 + d], gr.at[16 + d], a_dev[d]))
    t_step(2)
    for d, ka in ((0, 1), (1, 3)):
        part = gb_last(ka)
        rdma(rah.at[d], rah.at[d], gs.at[16 + d], gr.at[16 + d], sib).wait_recv()
        r1[1 + d, d] = (part[d] + rah[d].astype(f32)).astype(bf16)
        r1[1 + d, 1 - d] = part[1 - d].astype(bf16)
        go(rdma(r1.at[1 + d], raf.at[d], gs.at[18 + d], gr.at[18 + d], a_dev[d]))
    t_step(3)
    total = gb_last(0)
    for d in (0, 1):
        rdma(raf.at[d], raf.at[d], gs.at[18 + d], gr.at[18 + d], sib).wait_recv()
    total = total + raf[0].astype(f32) + raf[1].astype(f32)
    for c in (0, 1):
        fin[c] = total[:, c * PART:(c + 1) * PART]
    last = rdma(fin.at[1 - core], fin_in, xs.at[1], xr.at[1], sib)
    go(last)

    for d in (0, 1):
        t_copy(d, 3).wait_recv()
    txt = text_sum(0) + trecv[0, 3].astype(f32) + trecv[1, 3].astype(f32)
    txt_out[...] = txt.reshape(ROWS, D) * t_inv

    last.wait_recv()
    mine = fin[core]
    other = fin_in[...]
    even = jnp.where(first, mine, other)
    odd = jnp.where(first, other, mine)
    blocks = []
    for g in range(8):
        lo = (g % 4) * ROWS
        blocks += [even[g // 4][:, lo:lo + ROWS], odd[g // 4][:, lo:lo + ROWS]]
    img_out[...] = jnp.concatenate(blocks, axis=1).astype(bf16)

    for copy in started:
        copy.wait_send()


def local(picture_embeds, caption_embeds, positive_caption_ids, logit_multiplier, logit_shift):
    vmem = pl.BlockSpec(memory_space=pltpu.VMEM)
    smem = pl.BlockSpec(memory_space=pltpu.SMEM)
    dma = pltpu.SemaphoreType.DMA
    scratch = [
        pltpu.VMEM((16, 2, HALF, D), bf16),
        pltpu.VMEM((16, 8, 128), f32),
        pltpu.VMEM((16, 2, HALF, D), bf16),
        pltpu.VMEM((4, D, 256), bf16),
        pltpu.VMEM((D, 1024), bf16),
        pltpu.VMEM((1024, 1024), bf16),
        pltpu.VMEM((2, 512, 128), f32),
        pltpu.VMEM((4, 8, 256), f32),
        pltpu.VMEM((NZ, 2, HALF, D), f32),
        pltpu.VMEM((NZ, 2, HALF, D), bf16),
        pltpu.VMEM((NZ, 2, HALF, D), bf16),
        pltpu.VMEM((2, 4, 2, HALF, D), bf16),
        pltpu.VMEM((2, 4, 2, HALF, D), bf16),
        pltpu.VMEM((16, 2, FEAT, 256), bf16),
        pltpu.VMEM((4, 2, FEAT, 256), bf16),
        pltpu.VMEM((4, 2, 2, FEAT, 256), bf16),
        pltpu.VMEM((2, FEAT, 256), bf16),
        pltpu.VMEM((2, 2, FEAT, 256), bf16),
        pltpu.VMEM((3, 2, FEAT, 256), bf16),
        pltpu.VMEM((2, 2, PART, 256), f32),
        pltpu.VMEM((2, PART, 256), f32),
        dma((20,)), dma((20,)),
        dma((15,)), dma((15,)),
        dma((8,)), dma((8,)),
        dma((8,)), dma((8,)),
        dma((8,)), dma((8,)),
        dma((20,)), dma((20,)),
        dma((2,)), dma((2,)),
    ]
    return pl.pallas_call(
        kernel,
        out_shape=(jax.ShapeDtypeStruct((PART, 1024), bf16), jax.ShapeDtypeStruct((ROWS, D), f32)),
        in_specs=[vmem, vmem, vmem, smem, smem],
        out_specs=(vmem, vmem),
        scratch_shapes=scratch,
        compiler_params=pltpu.CompilerParams(
            collective_id=0, has_side_effects=True, vmem_limit_bytes=56 * 2**20),
        cost_estimate=pl.CostEstimate(flops=7 * 10**9, bytes_accessed=10**6, transcendentals=2**20),
    )(picture_embeds, caption_embeds, positive_caption_ids.reshape(1, ROWS), logit_multiplier, logit_shift)


def solution(mesh):
    placed = (P(("batch", "group"), None), P(("batch", "group"), None), P(("batch", "group")), P(), P())
    return jax.shard_map(
        local, mesh=mesh, in_specs=placed,
        out_specs=(P("group", "batch"), P(("batch", "group"), None)), check_vma=False)
```

time: 409 us -> 73.3 us (0.18)
  waiting for transfers between devices: 154 us -> 0 us
  matrix products: 153 us -> 0 us
  Pallas kernels: 0 us -> 68.9 us
  starting transfers between devices: 60.6 us -> 0 us
  between operations: 14.7 us -> 1.94 us
  blocking collectives: 10.8 us -> 0 us
  other arithmetic: 8.12 us -> 0 us
    dot_general x48 -> x0, matrix products: 153 us -> none  [the longest x16 82 us: tile_loss_entries(): jnp.dot(entry_factor, caption_slice, preferred_element_type=jnp.float32)]
    reduce_scatter x1 -> x0, waiting for transfers between devices: 80.8 us -> none  [local(): lax.psum_scatter(image_up, 'group', scatter_dimension=0, tiled=True)]
    pallas_call x0 -> x1, Pallas kernels: none -> 68.9 us  [local(): pl.pallas_call(kernel, out_shape=(jax.ShapeDtypeStruct((PART, 1024), bf16...]
    ppermute x32 -> x0, starting transfers between devices: 52.9 us -> none  [shifted(): lax.ppermute(shard, axis, [(i, (i + by) % size) for i in range(size)])]
    ppermute x32 -> x0, waiting for transfers between devices: 41.2 us -> none  [shifted(): lax.ppermute(shard, axis, [(i, (i + by) % size) for i in range(size)])]
    all_gather x1 -> x0, waiting for transfers between devices: 25.8 us -> none  [local(): lax.all_gather(own_unit, 'group', axis=0, tiled=True)]
    unnamed x1 -> x0, blocking collectives: 10.8 us -> none
    all_to_all x1 -> x0, starting transfers between devices: 7.52 us -> none  [local(): lax.all_to_all(image_back.T.astype(jnp.bfloat16), 'group', split_axis=0,...]
  transfers between devices with their start and end apart: 35 -> 0, of which waited for: 19 -> 0; matrix products, arithmetic and copies ran while one was open for 39% -> 0% of each run, Pallas kernels for 0% -> 0%
where the time goes in v1:
time: 73.3 us; the launch traced here: 73.2 us
  Pallas kernels  68.9 us (94%)
  local copies, waits for them, and re-layouts  2.34 us (3%)
  between operations  1.94 us (3%)
    pallas_call x1, Pallas kernels, local(): pl.pallas_call(kernel, out_shape=(jax.ShapeDtypeStruct((PART, 1024), bf16...  68.9 us
    unnamed x4, local copies, waits for them, and re-layouts  2.34 us

profile of v1, /device:TPU:1, one launch (start us, length us, event | category | flops | bytes accessed | tf_op | source)
XLA Modules:
  0.0 73.2 jit_solution(5485280034463038597)
XLA Ops:
  1.9 68.9 %shard_map.68 = (bf16[72,1024]{1,0:T(8,128)(2,1)}, f32[64,1152]{1,0:T(8,128)}) custom-call(bf16[64,1152]{1,0:T(8,128)(2,1)} %pic.1, bf16[64,1152]{1,0:T(8,128)(2,1)} %cap.1, s32[1,64]{1,0:T(1,128)} %bitcast.1, f32[1]{0:T(128)S(6)} %copy.9.mul, f32[1]{0:T(128)S(6)} %copy.10.shift), custom_call_target="tpu_custom_call" | custom-call | flops 7000000000 | bytes 1000000 | tf_op jit(solution)/shard_map/pallas_call | solution.py:384
  70.8 0.0 copy-start
  70.8 1.6 %copy.11 = bf16[72,1024]{1,0:T(8,128)(2,1)} copy(bf16[72,1024]{1,0:T(8,128)(2,1)} %get-tuple-element.4) | data formatting | bytes 294912
  72.4 0.0 copy-done
  72.4 0.7 copy.12
Async XLA Ops:
  70.8 1.6 %copy-start = (f32[64,1152]{1,0:T(8,128)S(1)}, f32[64,1152]{1,0:T(8,128)}, u32[]{:S(2)}) copy-start(f32[64,1152]{1,0:T(8,128)} %get-tuple-element.5) | copy-start | bytes 884740

commit v2 on v0

v2 whole, which is shorter than its diff:
```python
import functools

import jax
import jax.numpy as jnp
from jax import lax
from jax.experimental import pallas as pl
from jax.experimental.pallas import tpu as pltpu
from jax.sharding import PartitionSpec as P

EPS = 1e-06
ROWS = 64
HALF = ROWS // 2
D = 1152
SIDE = 4
NZ = 8
FEAT = D // 8
PART = D // 16
LOG2E = 1.4426950408889634
f32 = jnp.float32
bf16 = jnp.bfloat16


def rdma(src, dst, ssem, rsem, dev):
    return pltpu.make_async_remote_copy(
        src_ref=src, dst_ref=dst, send_sem=ssem, recv_sem=rsem,
        device_id=dev, device_id_type=pl.DeviceIdType.MESH)


def unit_rows(values):
    wide = values.astype(f32)
    inverse = lax.rsqrt(jnp.sum(wide * wide, axis=1, keepdims=True) + EPS)
    return wide * inverse, inverse
VMEM_MIB = 48

ORDER = (4, 3, 5, 2, 6, 1, 7, 0)
PLACE = {k: i for i, k in enumerate(ORDER)}
N_SEM = 160


def kernel(pic_hbm, cap_hbm, lab, mul, shift, img_out, txt_out,
           pic, cap, U, M, T, Ut, Tt, W, tacc, svec, own, sib_out, sib_in,
           tstage, trecv, G, rbh, rbf, ra, r1, fin, fin_in, ssem, rsem, lsem):
    batch = lax.axis_index("batch")
    group = lax.axis_index("group")
    z, yh = batch // 2, batch % 2
    core = group % 2
    x = (group // 2) % SIDE
    y = yh * 2 + group // (2 * SIDE)
    m = mul[0]
    shift0 = shift[0]
    first = core == 0
    pa = jnp.where(first, x, y)
    pb = jnp.where(first, y, x)

    def dev(x_, y_, z_, c_):
        return (z_ * 2 + y_ // 2, ((y_ % 2) * SIDE + x_) * 2 + c_)

    def slot(ka, kb):
        return (pb + kb) % SIDE * SIDE + (pa + ka) % SIDE

    def plane(ka, kb):
        a_ = (pa + ka) % SIDE
        b_ = (pb + kb) % SIDE
        return dev(jnp.where(first, a_, b_), jnp.where(first, b_, a_), z, core)

    z_dev = (dev(x, y, (z + 1) % NZ, core), dev(x, y, (z + NZ - 1) % NZ, core))
    b_dev = (plane(0, 1), plane(0, SIDE - 1))
    sib = dev(x, y, z, 1 - core)

    loads = (pltpu.make_async_copy(pic_hbm, pic, lsem.at[0]),
             pltpu.make_async_copy(cap_hbm, cap, lsem.at[1]))
    for load in loads:
        load.start()
    barrier = pltpu.get_barrier_semaphore()
    partners = (*z_dev, *b_dev, plane(1, 0), plane(3, 0), plane(2, 0), sib)
    for d in partners:
        pl.semaphore_signal(barrier, inc=1, device_id=d, device_id_type=pl.DeviceIdType.MESH)

    table = {}
    started = []

    def at(key):
        i = table.setdefault(key, len(table))
        assert i < N_SEM
        return i

    def send(key, src, dst, to):
        copy = rdma(src, dst, ssem.at[at(key)], rsem.at[at(key)], to)
        copy.start()
        started.append(copy)

    def got(key, dst):
        rdma(dst, dst, ssem.at[at(key)], rsem.at[at(key)], sib).wait_recv()

    me = slot(0, 0)
    loads[1].wait()
    t_unit, t_inv = unit_rows(cap[...])
    T[PLACE[0]] = t_unit.astype(bf16).reshape(2, HALF, D)
    loads[0].wait()
    p_unit, p_inv = unit_rows(pic[...])
    U[me] = p_unit.astype(bf16).reshape(2, HALF, D)
    spread = jnp.broadcast_to(p_inv, (ROWS, 128))
    inv_lane = jnp.concatenate([spread, spread], axis=0).T[0:8]
    lab_row = lab[...].astype(f32)
    lab_lane = jnp.broadcast_to(jnp.concatenate([lab_row, lab_row], axis=1), (8, 128))
    row8 = lax.broadcasted_iota(jnp.int32, (8, 128), 0)
    lane8 = lax.broadcasted_iota(jnp.int32, (8, 128), 1)
    meta = jnp.where(row8 == 0, inv_lane, jnp.where(row8 == 1, lab_lane, 0.0))
    M[me] = jnp.where(lane8 // ROWS == pa % 2, meta, 0.0)

    pl.semaphore_wait(barrier, len(partners))

    def send_u(ka, kb, hf, da, db):
        s = slot(ka, kb)
        send(("u", (ka - da) % SIDE, (kb - db) % SIDE, hf), U.at[s, hf], U.at[s, hf], plane(da, db))

    def got_u(ka, kb, hf):
        got(("u", ka, kb, hf), U.at[slot(ka, kb), hf])

    def send_m(ka, kb, da, db):
        s = slot(ka, kb)
        send(("m", (ka - da) % SIDE, (kb - db) % SIDE), M.at[s], M.at[s], plane(da, db))

    def got_m(ka, kb):
        got(("m", ka, kb), M.at[slot(ka, kb)])

    def send_t(k, hf, d):
        to = (k + (NZ - 1 if d == 0 else 1)) % NZ
        send(("t", to, hf), T.at[PLACE[k], hf], T.at[PLACE[to], hf], z_dev[d])

    def got_t(k, hf):
        got(("t", k, hf), T.at[PLACE[k], hf])

    def to_sib(k):
        send(("ts", k), T.at[PLACE[k]], T.at[NZ + PLACE[k]], sib)

    def got_sib(k):
        got(("ts", k), T.at[NZ + PLACE[k]])

    for step in (0, 1):
        for d in (0, 1):
            hf = d ^ step
            send_t(0, hf, d)
            send_u(0, 0, hf, 0, (1, 3)[d])
            send_u(0, 0, hf, (1, 3)[d], 0)
    for hf in (0, 1):
        send_u(0, 0, hf, 2, 0)
    for to in ((1, 0), (3, 0), (2, 0), (0, 1), (0, 3)):
        send_m(0, 0, *to)
    to_sib(0)

    tacc[...] = jnp.zeros_like(tacc)
    svec[...] = jnp.zeros_like(svec)

    def fwd_b(ka, d):
        hf = d
        kb = (3, 1)[d]
        got_u(ka, kb, hf)
        send_u(ka, kb, hf, 0, (1, 3)[d])

    def along_b(ka, hf):
        got_u(ka, 0, hf)
        for d in ((0, 1) if hf == 0 else (1, 0)):
            send_u(ka, 0, hf, 0, (1, 3)[d])

    def meta_b(ka):
        got_m(ka, 0)
        send_m(ka, 0, 0, 1)
        send_m(ka, 0, 0, 3)

    def rest_b(ka):
        got_u(ka, 3, 1)
        got_u(ka, 1, 0)
        got_m(ka, 3)
        send_m(ka, 3, 0, 1)
        got_m(ka, 1)

    def last_b(ka):
        got_u(ka, 2, 0)
        got_u(ka, 2, 1)
        got_m(ka, 2)

    got_t(7, 0)
    send_t(7, 0, 0)
    got_t(1, 1)
    send_t(1, 1, 1)
    fwd_b(0, 0)
    fwd_b(0, 1)
    along_b(3, 0)
    along_b(1, 1)
    got_t(7, 1)
    send_t(7, 1, 0)
    got_t(1, 0)
    send_t(1, 0, 1)
    along_b(3, 1)
    along_b(1, 0)
    to_sib(7)
    to_sib(1)
    along_b(2, 0)
    along_b(2, 1)
    meta_b(3)
    meta_b(1)
    meta_b(2)
    rest_b(0)
    got_t(6, 0)
    send_t(6, 0, 0)
    got_t(2, 1)
    send_t(2, 1, 1)
    for ka in (3, 1):
        fwd_b(ka, 0)
        fwd_b(ka, 1)
    got_t(6, 1)
    send_t(6, 1, 0)
    got_t(2, 0)
    send_t(2, 0, 1)
    to_sib(6)
    to_sib(2)

    base = yh * 1024 + (group // 2) * 128
    k1 = m * LOG2E
    k2 = shift0 * LOG2E

    def lane_vec(v, r):
        return M[2 * v, r:r + 1] + M[2 * v + 1, r:r + 1]

    def transpose_texts(q):
        flipped = T[4 * q:4 * q + 4].reshape(256, D).T
        Tt[:, :, q * 256:(q + 1) * 256] = flipped.reshape(8, FEAT, 256)

    def transpose_images(kb):
        b_ = (pb + kb) % SIDE
        flipped = U[pl.ds(b_ * SIDE, SIDE)].reshape(256, D).T
        for i in (0, 1):
            Ut[2 * b_ + i] = flipped[:, i * 128:(i + 1) * 128].reshape(8, FEAT, 128)

    def weights(part, kb):
        b_ = (pb + kb) % SIDE
        images = U[pl.ds(b_ * SIDE, SIDE)].reshape(256, D)
        label = jnp.concatenate([lane_vec(2 * b_, 1), lane_vec(2 * b_ + 1, 1)], axis=1)
        row = lax.broadcasted_iota(jnp.int32, (ROWS, 1), 0)
        for side in (0, 1):
            rows = T[pl.ds(side * NZ + part * 4, 4)].reshape(256, D)
            cos = lax.dot_general(rows, images, (((1,), (1,)), ((), ())), preferred_element_type=f32)
            owner = core if side == 0 else 1 - core
            ids = []
            for j in range(4):
                k = jnp.where(part == 0, ORDER[j], ORDER[4 + j])
                ids.append(row + ((z + k) % NZ * 2048 + base + owner * ROWS))
            match = jnp.concatenate(ids, axis=0).astype(f32) == label
            logit = cos * k1 + k2
            e = jnp.exp2(jnp.where(match, logit, -logit))
            w = (jnp.where(match, -m, m) / (1.0 + e)).astype(bf16)
            at_row = pl.ds(pl.multiple_of(side * 512 + part * 256, 256), 256)
            wc = w.astype(f32) * cos
            total = jnp.sum(wc, axis=0, keepdims=True)
            for i in (0, 1):
                cut = slice(i * 128, (i + 1) * 128)
                W[2 * b_ + i, at_row] = w[:, cut]
                svec[2 * b_ + i] += jnp.broadcast_to(total[:, cut], (8, 128))
            tacc[side * 2 + part] += wc[:, :128] + wc[:, 128:]

    for k in (0, 7, 1, 6):
        got_sib(k)
    weights(1, 0)
    got_t(5, 0)
    send(("t", 4, 0), T.at[PLACE[5], 0], T.at[PLACE[4], 0], z_dev[0])
    got_t(3, 1)
    send(("t", 4, 1), T.at[PLACE[3], 1], T.at[PLACE[4], 1], z_dev[1])
    fwd_b(2, 0)
    fwd_b(2, 1)
    got_t(5, 1)
    got_t(3, 0)
    to_sib(5)
    to_sib(3)
    for ka in (3, 1, 2):
        rest_b(ka)

    @pl.loop(0, 2)
    def _(i):
        weights(1, 1 + 2 * i)

    transpose_texts(1)
    transpose_texts(3)
    for kb in (0, 1, 3):
        transpose_images(kb)

    for ka in (0, 3, 1, 2):
        last_b(ka)
    got_t(4, 0)
    got_t(4, 1)
    to_sib(4)
    weights(1, 2)
    for k in (2, 5, 3, 4):
        got_sib(k)

    @pl.loop(0, 4)
    def _(i):
        weights(0, i)

    transpose_texts(0)
    transpose_texts(2)
    transpose_images(2)

    def text_part(q):
        lhs = jnp.concatenate([W[u, q * 256:(q + 1) * 256] for u in range(8)], axis=1)
        up = jnp.dot(lhs, U[...].reshape(1024, D), preferred_element_type=f32)
        along = jnp.sum(tacc[q], axis=1, keepdims=True)
        return (up - T[4 * q:4 * q + 4].reshape(256, D).astype(f32) * along).reshape(4, 2, HALF, D)

    def sib_part(part):
        sib_out[part] = text_part(2 + part).astype(bf16)
        send(("s", part), sib_out.at[part], sib_in.at[part], sib)

    def own_part(part):
        own[part] = text_part(part)

    def image_part(kb):
        b_ = (pb + kb) % SIDE

        @pl.loop(0, 2)
        def _(u):
            h = jnp.where(first, b_ // 2, u)
            units = [jnp.where(first, 4 * h + i, 2 * i + h) for i in range(4)]
            gs = [jnp.where(first, b_ % 2 * 4 + 2 * u + j, j * 4 + b_) for j in (0, 1)]
            lhs = jnp.concatenate([Tt[g] for g in gs], axis=0)
            rhs = jnp.concatenate([W[v] for v in units], axis=1)
            up = jnp.dot(lhs, rhs, preferred_element_type=f32)
            for hf in (0, 1):
                pair = units[2 * hf:2 * hf + 2]
                along = jnp.concatenate([svec[v][0:1] for v in pair], axis=1)
                inv = jnp.concatenate([lane_vec(v, 0) for v in pair], axis=1)
                for j, g in enumerate(gs):
                    unit = jnp.concatenate([Ut[v, g] for v in pair], axis=1).astype(f32)
                    part = up[j * FEAT:(j + 1) * FEAT, hf * 256:(hf + 1) * 256]
                    G[kb, 2 * u + j, hf] = ((part - unit * along) * inv).astype(bf16)

    A_ORDER = (2, 1, 3, 0)

    def a_at(ka):
        return (pa + ka) % SIDE

    def gb_far():
        for ka in A_ORDER:
            for d in (0, 1):
                send(("gh", ka, d), G.at[2, a_at(ka), d], rbh.at[ka, d], b_dev[d])

    def gb_near(d, fresh):
        kb = (1, 3)[d]
        for ka in A_ORDER:
            hf = 1 - d if fresh else d
            if not fresh:
                got(("gh", ka, d), rbh.at[ka, d])
                G[kb, a_at(ka), hf] = (G[kb, a_at(ka), hf].astype(f32) + rbh[ka, d].astype(f32)).astype(bf16)
            send(("gf", ka, d, hf), G.at[kb, a_at(ka), hf], rbf.at[ka, d, hf], b_dev[d])

    def gb_sum(ka):
        for d in (0, 1):
            for hf in (0, 1):
                got(("gf", ka, d, hf), rbf.at[ka, d, hf])
        return G[0, a_at(ka)].astype(f32) + rbf[ka, 0].astype(f32) + rbf[ka, 1].astype(f32)

    def text_sum(k, hf):
        p = PLACE[k]
        return own[p // 4, p % 4, hf] + sib_in[p // 4, p % 4, hf].astype(f32)

    def text_step(i, d, hf):
        k = (4 - i if d == 0 else 4 + i) % NZ
        value = text_sum(k, hf)
        if i > 1 or (i == 1 and hf == d):
            got(("r", d, i - 1, hf), trecv.at[d, i - 1, hf])
            value = value + trecv[d, i - 1, hf].astype(f32)
        tstage[d, i, hf] = value.astype(bf16)
        send(("r", d, i, hf), tstage.at[d, i, hf], trecv.at[d, i, hf], z_dev[d])

    image_part(2)
    gb_far()
    sib_part(0)
    own_part(0)
    got(("s", 0), sib_in.at[0])
    text_step(0, 0, 0)
    text_step(0, 1, 1)
    text_step(1, 0, 1)
    text_step(1, 1, 0)
    image_part(1)
    gb_near(0, True)
    image_part(3)
    gb_near(1, True)
    gb_near(0, False)
    gb_near(1, False)
    text_step(1, 0, 0)
    text_step(1, 1, 1)
    sib_part(1)
    text_step(2, 0, 1)
    own_part(1)
    got(("s", 1), sib_in.at[1])
    text_step(2, 1, 0)
    image_part(0)
    text_step(2, 0, 0)
    text_step(2, 1, 1)
    for ka in (2, 1, 3):
        r1[ka - 1] = gb_sum(ka).astype(bf16)
        send(("ga", ka), r1.at[ka - 1], ra.at[ka - 1], plane(ka, 0))
    text_step(3, 0, 1)
    text_step(3, 1, 0)
    text_step(3, 0, 0)
    text_step(3, 1, 1)
    total = gb_sum(0)
    for ka in (1, 3, 2):
        got(("ga", ka), ra.at[ka - 1])
        total = total + ra[ka - 1].astype(f32)
    for c in (0, 1):
        fin[c] = total[:, c * PART:(c + 1) * PART]
    send(("x",), fin.at[1 - core], fin_in, sib)

    for hf in (0, 1):
        value = text_sum(0, hf)
        for d in (0, 1):
            got(("r", d, 3, hf), trecv.at[d, 3, hf])
            value = value + trecv[d, 3, hf].astype(f32)
        txt_out[hf * HALF:(hf + 1) * HALF] = value * t_inv[hf * HALF:(hf + 1) * HALF]

    got(("x",), fin_in)
    mine = fin[core]
    other = fin_in[...]
    even = jnp.where(first, mine, other)
    odd = jnp.where(first, other, mine)
    blocks = []
    for g in range(8):
        for half, j in ((even, g), (odd, g % 4 * 2 + g // 4)):
            lo = (j % 4) * ROWS
            blocks.append(half[j // 4][:, lo:lo + ROWS])
    img_out[...] = jnp.concatenate(blocks, axis=1).astype(bf16)

    for copy in started:
        copy.wait_send()


def local(picture_embeds, caption_embeds, positive_caption_ids, logit_multiplier, logit_shift):
    vmem = pl.BlockSpec(memory_space=pltpu.VMEM)
    hbm = pl.BlockSpec(memory_space=pl.ANY)
    smem = pl.BlockSpec(memory_space=pltpu.SMEM)
    dma = pltpu.SemaphoreType.DMA
    scratch = [
        pltpu.VMEM((ROWS, D), bf16),
        pltpu.VMEM((ROWS, D), bf16),
        pltpu.VMEM((16, 2, HALF, D), bf16),
        pltpu.VMEM((16, 8, 128), f32),
        pltpu.VMEM((16, 2, HALF, D), bf16),
        pltpu.VMEM((8, 8, FEAT, 128), bf16),
        pltpu.VMEM((8, FEAT, 1024), bf16),
        pltpu.VMEM((8, 1024, 128), bf16),
        pltpu.VMEM((4, 256, 128), f32),
        pltpu.VMEM((8, 8, 128), f32),
        pltpu.VMEM((2, 4, 2, HALF, D), f32),
        pltpu.VMEM((2, 4, 2, HALF, D), bf16),
        pltpu.VMEM((2, 4, 2, HALF, D), bf16),
        pltpu.VMEM((2, 4, 2, HALF, D), bf16),
        pltpu.VMEM((2, 4, 2, HALF, D), bf16),
        pltpu.VMEM((4, 4, 2, FEAT, 256), bf16),
        pltpu.VMEM((4, 2, FEAT, 256), bf16),
        pltpu.VMEM((4, 2, 2, FEAT, 256), bf16),
        pltpu.VMEM((3, 2, FEAT, 256), bf16),
        pltpu.VMEM((3, 2, FEAT, 256), bf16),
        pltpu.VMEM((2, 2, PART, 256), f32),
        pltpu.VMEM((2, PART, 256), f32),
        dma((N_SEM,)), dma((N_SEM,)), dma((2,)),
    ]
    return pl.pallas_call(
        kernel,
        out_shape=(jax.ShapeDtypeStruct((PART, 1024), bf16), jax.ShapeDtypeStruct((ROWS, D), f32)),
        in_specs=[hbm, hbm, vmem, smem, smem],
        out_specs=(vmem, vmem),
        scratch_shapes=scratch,
        compiler_params=pltpu.CompilerParams(
            collective_id=0, has_side_effects=True, vmem_limit_bytes=VMEM_MIB * 2**20),
        cost_estimate=pl.CostEstimate(flops=7 * 10**9, bytes_accessed=10**6, transcendentals=2**20),
    )(picture_embeds, caption_embeds, positive_caption_ids.reshape(1, ROWS), logit_multiplier, logit_shift)


def solution(mesh):
    placed = (P(("batch", "group"), None), P(("batch", "group"), None), P(("batch", "group")), P(), P())
    return jax.shard_map(
        local, mesh=mesh, in_specs=placed,
        out_specs=(P("group", "batch"), P(("batch", "group"), None)), check_vma=False)
```

time: 409 us -> 61.7 us (0.15)
  waiting for transfers between devices: 154 us -> 0 us
  matrix products: 153 us -> 0 us
  starting transfers between devices: 60.6 us -> 0 us
  Pallas kernels: 0 us -> 55.8 us
  between operations: 14.7 us -> 1.94 us
  blocking collectives: 10.8 us -> 0 us
  other arithmetic: 8.12 us -> 0 us
    dot_general x48 -> x0, matrix products: 153 us -> none  [the longest x16 82 us: tile_loss_entries(): jnp.dot(entry_factor, caption_slice, preferred_element_type=jnp.float32)]
    reduce_scatter x1 -> x0, waiting for transfers between devices: 80.8 us -> none  [local(): lax.psum_scatter(image_up, 'group', scatter_dimension=0, tiled=True)]
    pallas_call x0 -> x1, Pallas kernels: none -> 55.8 us  [local(): pl.pallas_call(kernel, out_shape=(jax.ShapeDtypeStruct((PART, 1024), bf16...]
    ppermute x32 -> x0, starting transfers between devices: 52.9 us -> none  [shifted(): lax.ppermute(shard, axis, [(i, (i + by) % size) for i in range(size)])]
    ppermute x32 -> x0, waiting for transfers between devices: 41.2 us -> none  [shifted(): lax.ppermute(shard, axis, [(i, (i + by) % size) for i in range(size)])]
    all_gather x1 -> x0, waiting for transfers between devices: 25.8 us -> none  [local(): lax.all_gather(own_unit, 'group', axis=0, tiled=True)]
    unnamed x1 -> x0, blocking collectives: 10.8 us -> none
    all_to_all x1 -> x0, starting transfers between devices: 7.52 us -> none  [local(): lax.all_to_all(image_back.T.astype(jnp.bfloat16), 'group', split_axis=0,...]
  transfers between devices with their start and end apart: 35 -> 0, of which waited for: 19 -> 0; matrix products, arithmetic and copies ran while one was open for 39% -> 0% of each run, Pallas kernels for 0% -> 0%
where the time goes in v2:
time: 61.7 us; the launch traced here: 61.6 us
  Pallas kernels  55.8 us (90%)
  local copies, waits for them, and re-layouts  3.84 us (6%)
  between operations  1.94 us (3%)
    pallas_call x1, Pallas kernels, local(): pl.pallas_call(kernel, out_shape=(jax.ShapeDtypeStruct((PART, 1024), bf16...  55.8 us
    unnamed x8, local copies, waits for them, and re-layouts  3.84 us

profile of v2, /device:TPU:1, one launch (start us, length us, event | category | flops | bytes accessed | tf_op | source)
XLA Modules:
  0.0 61.6 jit_solution(17889479889955402620)
XLA Ops:
  1.9 0.0 copy-start.2
  1.9 0.6 %copy-done.2 = s32[64]{0:T(128)S(1)} copy-done((s32[64]{0:T(128)S(1)}, s32[64]{0:T(128)}, u32[]{:S(2)}) %copy-start.2) | copy-done | bytes 280
  2.6 0.0 copy-start
  2.6 0.9 %copy-done = bf16[64,1152]{1,0:T(8,128)(2,1)S(1)} copy-done((bf16[64,1152]{1,0:T(8,128)(2,1)S(1)}, bf16[64,1152]{1,0:T(8,128)(2,1)}, u32[]{:S(2)}) %copy-start) | copy-done | bytes 147480
  3.5 0.0 copy-start.1
  3.5 0.9 %copy-done.1 = bf16[64,1152]{1,0:T(8,128)(2,1)S(1)} copy-done((bf16[64,1152]{1,0:T(8,128)(2,1)S(1)}, bf16[64,1152]{1,0:T(8,128)(2,1)}, u32[]{:S(2)}) %copy-start.1) | copy-done | bytes 147480
  4.4 55.8 %shard_map.68 = (bf16[72,1024]{1,0:T(8,128)(2,1)S(1)}, f32[64,1152]{1,0:T(8,128)S(1)}) custom-call(bf16[64,1152]{1,0:T(8,128)(2,1)S(1)} %copy-done, bf16[64,1152]{1,0:T(8,128)(2,1)S(1)} %copy-done.1, s32[1,64]{1,0:T(1,128)S(1)} %bitcast.1, f32[1]{0:T(128)S(6)} %copy.9.mul, f32[1]{0:T(128)S(6)} %copy.10.shift), custom_call_target="tpu_custom_call" | custom-call | flops 7000000000 | bytes 1000000 | tf_op jit(solution)/shard_map/pallas_call | solution.py:468
  60.2 0.7 %copy.11 = bf16[72,1024]{1,0:T(8,128)(2,1)} copy(bf16[72,1024]{1,0:T(8,128)(2,1)S(1)} %get-tuple-element.4) | data formatting | bytes 294912
  60.9 0.7 %copy.12 = f32[64,1152]{1,0:T(8,128)} copy(f32[64,1152]{1,0:T(8,128)S(1)} %get-tuple-element.5) | data formatting | bytes 589824
Async XLA Ops:
  1.9 0.7 %copy-start.2 = (s32[64]{0:T(128)S(1)}, s32[64]{0:T(128)}, u32[]{:S(2)}) copy-start(s32[64]{0:T(128)} %param.7) | copy-start | bytes 772
  2.6 0.9 %copy-start = (bf16[64,1152]{1,0:T(8,128)(2,1)S(1)}, bf16[64,1152]{1,0:T(8,128)(2,1)}, u32[]{:S(2)}) copy-start(bf16[64,1152]{1,0:T(8,128)(2,1)} %pic_hbm.1) | copy-start | bytes 442372
  3.5 0.9 %copy-start.1 = (bf16[64,1152]{1,0:T(8,128)(2,1)S(1)}, bf16[64,1152]{1,0:T(8,128)(2,1)}, u32[]{:S(2)}) copy-start(bf16[64,1152]{1,0:T(8,128)(2,1)} %cap_hbm.1) | copy-start | bytes 442372

commit v3 on v2

v3 whole, which is shorter than its diff:
```python
import functools

import jax
import jax.numpy as jnp
from jax import lax
from jax.experimental import pallas as pl
from jax.experimental.pallas import tpu as pltpu
from jax.sharding import PartitionSpec as P

EPS = 1e-06
ROWS = 64
HALF = ROWS // 2
D = 1152
SIDE = 4
NZ = 8
FEAT = D // 8
PART = D // 16
PAD = 80
LOG2E = 1.4426950408889634
f32 = jnp.float32
bf16 = jnp.bfloat16


def rdma(src, dst, ssem, rsem, dev):
    return pltpu.make_async_remote_copy(
        src_ref=src, dst_ref=dst, send_sem=ssem, recv_sem=rsem,
        device_id=dev, device_id_type=pl.DeviceIdType.MESH)


def unit_rows(values):
    wide = values.astype(f32)
    inverse = lax.rsqrt(jnp.sum(wide * wide, axis=1, keepdims=True) + EPS)
    return wide * inverse, inverse
VMEM_MIB = 48

ORDER = (4, 3, 5, 2, 6, 1, 7, 0)
PLACE = {k: i for i, k in enumerate(ORDER)}
N_SEM = 160


def kernel(pic_hbm, cap_hbm, lab_hbm, mul, shift, img_out, txt_out,
           pic, cap, lab, U, M, T, Ut, Tt, W, tacc, svec, own, sib_out, sib_in,
           tstage, trecv, G, rbh, rbf, ra, ra_sib, r1, fin, ssem, rsem, lsem):
    batch = lax.axis_index("batch")
    group = lax.axis_index("group")
    z, yh = batch // 2, batch % 2
    core = group % 2
    x = (group // 2) % SIDE
    y = yh * 2 + group // (2 * SIDE)
    first = core == 0
    pa = jnp.where(first, x, y)
    pb = jnp.where(first, y, x)

    def dev(x_, y_, z_, c_):
        return (z_ * 2 + y_ // 2, ((y_ % 2) * SIDE + x_) * 2 + c_)

    def slot(ka, kb):
        return (pb + kb) % SIDE * SIDE + (pa + ka) % SIDE

    def plane(ka, kb, c_=core):
        a_ = (pa + ka) % SIDE
        b_ = (pb + kb) % SIDE
        return dev(jnp.where(first, a_, b_), jnp.where(first, b_, a_), z, c_)

    z_dev = (dev(x, y, (z + 1) % NZ, core), dev(x, y, (z + NZ - 1) % NZ, core))
    z_cross = (dev(x, y, (z + 1) % NZ, 1 - core), dev(x, y, (z + NZ - 1) % NZ, 1 - core))
    b_dev = (plane(0, 1), plane(0, SIDE - 1))
    sib = dev(x, y, z, 1 - core)

    loads = [pltpu.make_async_copy(src, dst, lsem.at[i]) for i, (src, dst) in enumerate(
        ((pic_hbm, pic), (cap_hbm, cap), (lab_hbm, lab)))]
    for load in loads:
        load.start()
    barrier = pltpu.get_barrier_semaphore()
    near = (*z_dev, *z_cross, *b_dev, plane(0, 2), plane(1, 0), plane(3, 0), plane(2, 0), sib)
    partners = (*near, *(plane(0, kb, 1 - core) for kb in (1, 2, 3)))
    for d in partners:
        pl.semaphore_signal(barrier, inc=1, device_id=d, device_id_type=pl.DeviceIdType.MESH)

    table = {}
    started = []

    def at(key):
        i = table.setdefault(key, len(table))
        assert i < N_SEM
        return i

    def send(key, src, dst, to):
        copy = rdma(src, dst, ssem.at[at(key)], rsem.at[at(key)], to)
        copy.start()
        started.append(copy)

    def got(key, dst):
        rdma(dst, dst, ssem.at[at(key)], rsem.at[at(key)], sib).wait_recv()

    me = slot(0, 0)
    loads[0].wait()
    p_unit, p_inv = unit_rows(pic[...])
    U[me] = p_unit.astype(bf16).reshape(2, HALF, D)

    def send_u(ka, kb, hf, da, db):
        s = slot(ka, kb)
        send(("u", (ka - da) % SIDE, (kb - db) % SIDE, hf), U.at[s, hf], U.at[s, hf], plane(da, db))

    def got_u(ka, kb, hf):
        got(("u", ka, kb, hf), U.at[slot(ka, kb), hf])

    def send_m(ka, kb, da, db):
        s = slot(ka, kb)
        send(("m", (ka - da) % SIDE, (kb - db) % SIDE), M.at[s], M.at[s], plane(da, db))

    def got_m(ka, kb):
        got(("m", ka, kb), M.at[slot(ka, kb)])

    def send_t(k, hf, d):
        to = (k + (NZ - 1 if d == 0 else 1)) % NZ
        send(("t", to, hf), T.at[PLACE[k], hf], T.at[PLACE[to], hf], z_dev[d])
        if to == NZ // 2:
            send(("tx", hf), T.at[PLACE[k], hf], T.at[NZ + PLACE[to], hf], z_cross[d])

    def got_t(k, hf):
        got(("t", k, hf), T.at[PLACE[k], hf])

    def got_t4():
        for hf in (0, 1):
            got_t(4, hf)
            got(("tx", hf), T.at[NZ + PLACE[4], hf])

    def to_sib(k):
        send(("ts", k), T.at[PLACE[k]], T.at[NZ + PLACE[k]], sib)

    def got_sib(k):
        got(("ts", k), T.at[NZ + PLACE[k]])

    pl.semaphore_wait(barrier, len(partners))
    for hf in (0, 1):
        send_u(0, 0, hf, 2, 0)
    loads[1].wait()
    t_unit, t_inv = unit_rows(cap[...])
    T[PLACE[0]] = t_unit.astype(bf16).reshape(2, HALF, D)
    for step in (0, 1):
        for d in (0, 1):
            send_t(0, d ^ step, d)
    for step in (0, 1):
        for d in (0, 1):
            send_u(0, 0, d ^ step, (1, 3)[d], 0)
    loads[2].wait()
    spread = jnp.broadcast_to(p_inv, (ROWS, 128))
    inv_lane = jnp.concatenate([spread, spread], axis=0).T[0:8]
    lab_row = lab[...].astype(f32)
    lab_lane = jnp.broadcast_to(jnp.concatenate([lab_row, lab_row], axis=1), (8, 128))
    row8 = lax.broadcasted_iota(jnp.int32, (8, 128), 0)
    lane8 = lax.broadcasted_iota(jnp.int32, (8, 128), 1)
    meta = jnp.where(row8 == 0, inv_lane, jnp.where(row8 == 1, lab_lane, 0.0))
    M[me] = jnp.where(lane8 // ROWS == pa % 2, meta, 0.0)
    for to in ((2, 0), (1, 0), (3, 0), (0, 2), (0, 1), (0, 3)):
        send_m(0, 0, *to)
    to_sib(0)
    for step in (0, 1):
        for d in (0, 1):
            send_u(0, 0, d ^ step, 0, (1, 3)[d])

    tacc[...] = jnp.zeros_like(tacc)
    svec[...] = jnp.zeros_like(svec)

    def fwd_b(ka, d):
        hf = d
        kb = (3, 1)[d]
        got_u(ka, kb, hf)
        send_u(ka, kb, hf, 0, (1, 3)[d])

    def along_b(ka, hf):
        got_u(ka, 0, hf)
        for d in ((0, 1) if hf == 0 else (1, 0)):
            send_u(ka, 0, hf, 0, (1, 3)[d])

    def meta_b(ka):
        got_m(ka, 0)
        for kb in (2, 1, 3):
            send_m(ka, 0, 0, kb)

    def row(kb):
        for ka in range(SIDE):
            if kb == 2:
                got_u(ka, 2, 0)
                got_u(ka, 2, 1)
            elif kb:
                got_u(ka, kb, 1 if kb == 3 else 0)
            if kb:
                got_m(ka, kb)

    m = mul[0]
    shift0 = shift[0]
    base = yh * 1024 + (group // 2) * 128
    k1 = m * LOG2E
    k2 = shift0 * LOG2E

    def lane_vec(v, r):
        return M[2 * v, r:r + 1] + M[2 * v + 1, r:r + 1]

    def transpose_texts(place, n):
        for side in (0, NZ):
            lo = (side + place) * ROWS
            flipped = T[side + place:side + place + n].reshape(n * ROWS, D).T
            Tt[:, :, lo:lo + n * ROWS] = flipped.reshape(8, FEAT, n * ROWS)

    def transpose_images(kb):
        b_ = (pb + kb) % SIDE
        flipped = U[pl.ds(b_ * SIDE, SIDE)].reshape(256, D).T
        for i in (0, 1):
            Ut[2 * b_ + i] = flipped[:, i * 128:(i + 1) * 128].reshape(8, FEAT, 128)

    def weights(place, n, kb):
        b_ = (pb + kb) % SIDE
        images = U[pl.ds(b_ * SIDE, SIDE)].reshape(256, D)
        label = jnp.concatenate([lane_vec(2 * b_, 1), lane_vec(2 * b_ + 1, 1)], axis=1)
        row = lax.broadcasted_iota(jnp.int32, (ROWS, 1), 0)
        size = n * ROWS
        for side in (0, 1):
            lo = (side * NZ + place) * ROWS
            rows = T[side * NZ + place:side * NZ + place + n].reshape(size, D)
            cos = lax.dot_general(rows, images, (((1,), (1,)), ((), ())), preferred_element_type=f32)
            owner = core if side == 0 else 1 - core
            ids = []
            for k in ORDER[place:place + n]:
                ids.append(row + ((z + k) % NZ * 2048 + base + owner * ROWS))
            match = jnp.concatenate(ids, axis=0).astype(f32) == label
            logit = cos * k1 + k2
            e = jnp.exp2(jnp.where(match, logit, -logit))
            w = (jnp.where(match, -m, m) / (1.0 + e)).astype(bf16)
            wc = w.astype(f32) * cos
            total = jnp.sum(wc, axis=0, keepdims=True)
            for i in (0, 1):
                cut = slice(i * 128, (i + 1) * 128)
                W[2 * b_ + i, lo:lo + size] = w[:, cut]
                svec[2 * b_ + i] += jnp.broadcast_to(total[:, cut], (8, 128))
            tacc[lo:lo + size] += wc[:, :128] + wc[:, 128:]

    along_b(2, 0)
    got_t(7, 0)
    send_t(7, 0, 0)
    got_t(1, 1)
    send_t(1, 1, 1)
    along_b(3, 0)
    along_b(1, 1)
    got_t(7, 1)
    send_t(7, 1, 0)
    got_t(1, 0)
    send_t(1, 0, 1)
    fwd_b(0, 0)
    fwd_b(0, 1)
    to_sib(7)
    to_sib(1)
    along_b(2, 1)
    meta_b(2)
    along_b(3, 1)
    along_b(1, 0)
    meta_b(1)
    meta_b(3)
    got_sib(1)
    got_sib(7)
    got_sib(0)
    row(0)
    weights(5, 3, 0)
    got_t(6, 0)
    send_t(6, 0, 0)
    got_t(2, 1)
    send_t(2, 1, 1)
    fwd_b(2, 0)
    transpose_texts(5, 3)
    transpose_images(0)
    fwd_b(3, 0)
    got_t(6, 1)
    send_t(6, 1, 0)
    got_t(2, 0)
    send_t(2, 0, 1)
    to_sib(6)
    fwd_b(1, 1)
    to_sib(2)
    got_sib(2)
    got_sib(6)
    weights(3, 2, 0)
    transpose_texts(3, 2)
    fwd_b(2, 1)
    got_t(5, 0)
    send_t(5, 0, 0)
    got_t(3, 1)
    send_t(3, 1, 1)
    fwd_b(3, 1)
    fwd_b(1, 0)
    row(1)
    got_t(5, 1)
    to_sib(5)
    got_t(3, 0)
    to_sib(3)
    row(3)
    weights(5, 3, 1)
    weights(5, 3, 3)
    weights(3, 2, 1)
    weights(3, 2, 3)
    transpose_images(1)
    transpose_images(3)
    row(2)
    weights(5, 3, 2)
    weights(3, 2, 2)
    transpose_images(2)
    got_t4()
    got_sib(3)
    got_sib(5)
    weights(0, 3, 0)
    weights(0, 3, 1)
    weights(0, 3, 2)
    weights(0, 3, 3)
    transpose_texts(0, 3)

    def text_part(place, n):
        rows = slice(place * ROWS, (place + n) * ROWS)
        lhs = jnp.concatenate([W[u, rows] for u in range(8)], axis=1)
        up = jnp.dot(lhs, U[...].reshape(1024, D), preferred_element_type=f32)
        along = jnp.sum(tacc[rows], axis=1, keepdims=True)
        unit = T[place:place + n].reshape(n * ROWS, D).astype(f32)
        return (up - unit * along).reshape(n, 2, HALF, D)

    def sib_part(place, n):
        cut = slice(place, place + n)
        sib_out[cut] = text_part(NZ + place, n).astype(bf16)
        send(("s", place), sib_out.at[cut], sib_in.at[cut], sib)

    def got_part(place, n):
        got(("s", place), sib_in.at[place:place + n])

    def own_part(place, n):
        own[place:place + n] = text_part(place, n)

    def image_part(kb, u):
        b_ = (pb + kb) % SIDE
        h = jnp.where(first, b_ // 2, u)
        units = [jnp.where(first, 4 * h + i, 2 * i + h) for i in range(4)]
        gs = [jnp.where(first, b_ % 2 * 4 + 2 * u + j, j * 4 + b_) for j in (0, 1)]
        lhs = jnp.concatenate([Tt[g] for g in gs], axis=0)
        rhs = jnp.concatenate([W[v] for v in units], axis=1)
        up = jnp.dot(lhs, rhs, preferred_element_type=f32)
        for hf in (0, 1):
            pair = units[2 * hf:2 * hf + 2]
            along = jnp.concatenate([svec[v][0:1] for v in pair], axis=1)
            inv = jnp.concatenate([lane_vec(v, 0) for v in pair], axis=1)
            for j, g in enumerate(gs):
                unit = jnp.concatenate([Ut[v, g] for v in pair], axis=1).astype(f32)
                part = up[j * FEAT:(j + 1) * FEAT, hf * 256:(hf + 1) * 256]
                G[kb, 2 * u + j, hf] = ((part - unit * along) * inv).astype(bf16)

    def a_at(ka):
        return (pa + ka) % SIDE

    def gb_far(ka):
        for d in (0, 1):
            send(("gh", ka, d), G.at[2, a_at(ka), d], rbh.at[ka, d], b_dev[d])

    def gb_near(d, ka, fresh):
        kb = (1, 3)[d]
        hf = 1 - d if fresh else d
        if not fresh:
            got(("gh", ka, d), rbh.at[ka, d])
            G[kb, a_at(ka), hf] = (G[kb, a_at(ka), hf].astype(f32) + rbh[ka, d].astype(f32)).astype(bf16)
        send(("gf", ka, d, hf), G.at[kb, a_at(ka), hf], rbf.at[ka, d, hf], b_dev[d])

    def gb_sum(ka):
        for d in (0, 1):
            for hf in (0, 1):
                got(("gf", ka, d, hf), rbf.at[ka, d, hf])
        return G[0, a_at(ka)].astype(f32) + rbf[ka, 0].astype(f32) + rbf[ka, 1].astype(f32)

    def text_sum(k, hf):
        p = PLACE[k]
        return own[p, hf] + sib_in[p, hf].astype(f32)

    def text_step(i, d, hf):
        k = (4 - i if d == 0 else 4 + i) % NZ
        value = text_sum(k, hf)
        if i > 1 or (i == 1 and hf == d):
            got(("r", d, i - 1, hf), trecv.at[d, i - 1, hf])
            value = value + trecv[d, i - 1, hf].astype(f32)
        tstage[d, i, hf] = value.astype(bf16)
        send(("r", d, i, hf), tstage.at[d, i, hf], trecv.at[d, i, hf], z_dev[d])

    def feature_halves(total, dst):
        for c in (0, 1):
            rows = jnp.concatenate([total[:, c * PART:(c + 1) * PART], jnp.zeros((2, PAD - PART, 256), f32)], axis=1)
            dst[c] = rows.astype(bf16)

    def along_a(ka):
        feature_halves(gb_sum(ka), r1.at[ka])
        i = at(("ga", 0, ka))
        at(("ga", 1, ka))
        for c in (0, 1):
            j = at(("ga to", c, ka))
            copy = rdma(r1.at[ka, c], ra.at[core, ka - 1], ssem.at[j], rsem.at[i + core], plane(ka, 0, c))
            copy.start()
            started.append(copy)

    def own_a():
        total = gb_sum(0)
        feature_halves(total, r1.at[0])
        for c in (0, 1):
            fin[c] = total[:, c * PART:(c + 1) * PART]
        send(("gs",), r1.at[0, 1 - core], ra_sib, sib)

    def image_end():
        got(("gs",), ra_sib)
        mine = fin[core]
        other = ra_sib[:, :PART].astype(f32)
        sums = [jnp.where(first, mine, other), jnp.where(first, other, mine)]
        for ka in (2, 1, 3):
            for c in (0, 1):
                got(("ga", c, ka), ra.at[c, ka - 1])
                sums[c] = sums[c] + ra[c, ka - 1, :, :PART].astype(f32)
        even, odd = sums
        blocks = []
        for g in range(8):
            for half, j in ((even, g), (odd, g % 4 * 2 + g // 4)):
                lo = (j % 4) * ROWS
                blocks.append(half[j // 4][:, lo:lo + ROWS])
        img_out[...] = jnp.concatenate(blocks, axis=1).astype(bf16)

    def text_end(hf):
        value = text_sum(0, hf)
        for d in (0, 1):
            got(("r", d, 3, hf), trecv.at[d, 3, hf])
            value = value + trecv[d, 3, hf].astype(f32)
        txt_out[hf * HALF:(hf + 1) * HALF] = value * t_inv[hf * HALF:(hf + 1) * HALF]

    u_far = (pa + 2) % SIDE // 2
    order = (2, 1, 3, 0)

    def image_parts(kb):
        @pl.loop(0, 2)
        def _(u):
            image_part(kb, u)

    image_part(2, u_far)
    gb_far(2)
    sib_part(0, 3)
    image_part(2, 1 - u_far)
    for ka in (1, 3, 0):
        gb_far(ka)
    own_part(0, 3)
    got_part(0, 3)
    text_step(0, 0, 0)
    text_step(0, 1, 1)
    text_step(1, 0, 1)
    text_step(1, 1, 0)
    image_parts(1)
    for ka in order:
        gb_near(0, ka, True)
    image_parts(3)
    for ka in order:
        gb_near(1, ka, True)
    for ka in order:
        for d in (0, 1):
            gb_near(d, ka, False)
    text_step(1, 0, 0)
    text_step(1, 1, 1)
    sib_part(3, 5)
    own_part(3, 5)
    got_part(3, 5)
    text_step(2, 0, 1)
    text_step(2, 1, 0)
    image_parts(0)
    text_step(2, 0, 0)
    text_step(2, 1, 1)
    for ka in (2, 1, 3):
        along_a(ka)
    text_step(3, 0, 1)
    text_step(3, 1, 0)
    own_a()
    text_step(3, 0, 0)
    text_step(3, 1, 1)
    image_end()
    text_end(0)
    text_end(1)

    for copy in started:
        copy.wait_send()


def local(picture_embeds, caption_embeds, positive_caption_ids, logit_multiplier, logit_shift):
    vmem = pl.BlockSpec(memory_space=pltpu.VMEM)
    hbm = pl.BlockSpec(memory_space=pltpu.HBM)
    smem = pl.BlockSpec(memory_space=pltpu.SMEM)
    dma = pltpu.SemaphoreType.DMA
    scratch = [
        pltpu.VMEM((ROWS, D), bf16),
        pltpu.VMEM((ROWS, D), bf16),
        pltpu.VMEM((1, ROWS), jnp.int32),
        pltpu.VMEM((16, 2, HALF, D), bf16),
        pltpu.VMEM((16, 8, 128), f32),
        pltpu.VMEM((16, 2, HALF, D), bf16),
        pltpu.VMEM((8, 8, FEAT, 128), bf16),
        pltpu.VMEM((8, FEAT, 1024), bf16),
        pltpu.VMEM((8, 1024, 128), bf16),
        pltpu.VMEM((1024, 128), f32),
        pltpu.VMEM((8, 8, 128), f32),
        pltpu.VMEM((NZ, 2, HALF, D), f32),
        pltpu.VMEM((NZ, 2, HALF, D), bf16),
        pltpu.VMEM((NZ, 2, HALF, D), bf16),
        pltpu.VMEM((2, 4, 2, HALF, D), bf16),
        pltpu.VMEM((2, 4, 2, HALF, D), bf16),
        pltpu.VMEM((4, 4, 2, FEAT, 256), bf16),
        pltpu.VMEM((4, 2, FEAT, 256), bf16),
        pltpu.VMEM((4, 2, 2, FEAT, 256), bf16),
        pltpu.VMEM((2, 3, 2, PAD, 256), bf16),
        pltpu.VMEM((2, PAD, 256), bf16),
        pltpu.VMEM((4, 2, 2, PAD, 256), bf16),
        pltpu.VMEM((2, 2, PART, 256), f32),
        dma((N_SEM,)), dma((N_SEM,)), dma((3,)),
    ]
    return pl.pallas_call(
        kernel,
        out_shape=(jax.ShapeDtypeStruct((PART, 1024), bf16), jax.ShapeDtypeStruct((ROWS, D), f32)),
        in_specs=[hbm, hbm, hbm, smem, smem],
        out_specs=(vmem, vmem),
        scratch_shapes=scratch,
        compiler_params=pltpu.CompilerParams(
            collective_id=0, has_side_effects=True, vmem_limit_bytes=VMEM_MIB * 2**20),
        cost_estimate=pl.CostEstimate(flops=7 * 10**9, bytes_accessed=10**6, transcendentals=2**20),
    )(*(pltpu.with_memory_space_constraint(v, pltpu.HBM) for v in (
        picture_embeds, caption_embeds, positive_caption_ids.reshape(1, ROWS))), logit_multiplier, logit_shift)


def solution(mesh):
    placed = (P(("batch", "group"), None), P(("batch", "group"), None), P(("batch", "group")), P(), P())
    return jax.shard_map(
        local, mesh=mesh, in_specs=placed,
        out_specs=(P("group", "batch"), P(("batch", "group"), None)), check_vma=False)
```

time: 61.7 us -> 56.6 us (0.917)
  Pallas kernels: 55.8 us -> 53.2 us
  local copies, waits for them, and re-layouts: 3.84 us -> 1.38 us
    pallas_call x1, Pallas kernels: 55.8 us -> 53.2 us  [local(): pl.pallas_call(kernel, out_shape=(jax.ShapeDtypeStruct((PART, 1024), bf16...]
    unnamed x8 -> x2, local copies, waits for them, and re-layouts: 3.84 us -> 1.38 us
where the time goes in v3:
time: 56.6 us; the launch traced here: 56.5 us
  Pallas kernels  53.2 us (94%)
  between operations  1.93 us (3%)
  local copies, waits for them, and re-layouts  1.38 us (2%)
    pallas_call x1, Pallas kernels, local(): pl.pallas_call(kernel, out_shape=(jax.ShapeDtypeStruct((PART, 1024), bf16...  53.2 us
    unnamed x2, local copies, waits for them, and re-layouts  1.38 us

profile of v3, /device:TPU:1, one launch (start us, length us, event | category | flops | bytes accessed | tf_op | source)
XLA Modules:
  0.0 56.5 jit_solution(3856076909548119431)
XLA Ops:
  1.9 53.2 %shard_map.68 = (bf16[72,1024]{1,0:T(8,128)(2,1)S(1)}, f32[64,1152]{1,0:T(8,128)S(1)}) custom-call(bf16[64,1152]{1,0:T(8,128)(2,1)} %pic_hbm.1, bf16[64,1152]{1,0:T(8,128)(2,1)} %cap_hbm.1, s32[1,64]{1,0:T(1,128)} %bitcast.1, f32[1]{0:T(128)S(6)} %copy.9.mul, f32[1]{0:T(128)S(6)} %copy.10.shift), custom_call_target="tpu_custom_call" | custom-call | flops 7000000000 | bytes 1000000 | tf_op jit(solution)/shard_map/pallas_call | solution.py:517
  55.1 0.7 %copy.11 = bf16[72,1024]{1,0:T(8,128)(2,1)} copy(bf16[72,1024]{1,0:T(8,128)(2,1)S(1)} %get-tuple-element.4) | data formatting | bytes 294912
  55.8 0.7 %copy.12 = f32[64,1152]{1,0:T(8,128)} copy(f32[64,1152]{1,0:T(8,128)S(1)} %get-tuple-element.5) | data formatting | bytes 589824

commit v4 on v3

--- a/solution.py
+++ b/solution.py
@@ -94,10 +94,13 @@
         rdma(dst, dst, ssem.at[at(key)], rsem.at[at(key)], sib).wait_recv()
 
     me = slot(0, 0)
+    loads[1].wait()
+    t_unit, t_inv = unit_rows(cap[...])
+    T[PLACE[0]] = t_unit.astype(bf16).reshape(2, HALF, D)
     loads[0].wait()
     p_unit, p_inv = unit_rows(pic[...])
     U[me] = p_unit.astype(bf16).reshape(2, HALF, D)
-
+    pl.semaphore_wait(barrier, len(partners))
     def send_u(ka, kb, hf, da, db):
         s = slot(ka, kb)
         send(("u", (ka - da) % SIDE, (kb - db) % SIDE, hf), U.at[s, hf], U.at[s, hf], plane(da, db))
@@ -132,15 +135,11 @@
     def got_sib(k):
         got(("ts", k), T.at[NZ + PLACE[k]])
 
-    pl.semaphore_wait(barrier, len(partners))
+    for step in (0, 1):
+        for d in (0, 1):
+            send_t(0, d ^ step, d)
     for hf in (0, 1):
         send_u(0, 0, hf, 2, 0)
-    loads[1].wait()
-    t_unit, t_inv = unit_rows(cap[...])
-    T[PLACE[0]] = t_unit.astype(bf16).reshape(2, HALF, D)
-    for step in (0, 1):
-        for d in (0, 1):
-            send_t(0, d ^ step, d)
     for step in (0, 1):
         for d in (0, 1):
             send_u(0, 0, d ^ step, (1, 3)[d], 0)
@@ -236,63 +235,63 @@
                 svec[2 * b_ + i] += jnp.broadcast_to(total[:, cut], (8, 128))
             tacc[lo:lo + size] += wc[:, :128] + wc[:, 128:]
 
-    along_b(2, 0)
     got_t(7, 0)
     send_t(7, 0, 0)
     got_t(1, 1)
     send_t(1, 1, 1)
-    along_b(3, 0)
-    along_b(1, 1)
     got_t(7, 1)
     send_t(7, 1, 0)
     got_t(1, 0)
     send_t(1, 0, 1)
+    to_sib(7)
+    to_sib(1)
+    along_b(3, 0)
+    along_b(1, 1)
+    along_b(2, 0)
+    along_b(2, 1)
     fwd_b(0, 0)
     fwd_b(0, 1)
-    to_sib(7)
-    to_sib(1)
-    along_b(2, 1)
-    meta_b(2)
     along_b(3, 1)
     along_b(1, 0)
+    meta_b(2)
     meta_b(1)
     meta_b(3)
+    got_t(6, 0)
+    send_t(6, 0, 0)
+    got_t(2, 1)
+    send_t(2, 1, 1)
+    got_t(6, 1)
+    send_t(6, 1, 0)
+    got_t(2, 0)
+    send_t(2, 0, 1)
+    to_sib(6)
+    to_sib(2)
     got_sib(1)
     got_sib(7)
     got_sib(0)
     row(0)
     weights(5, 3, 0)
-    got_t(6, 0)
-    send_t(6, 0, 0)
-    got_t(2, 1)
-    send_t(2, 1, 1)
     fwd_b(2, 0)
-    transpose_texts(5, 3)
-    transpose_images(0)
+    fwd_b(2, 1)
     fwd_b(3, 0)
-    got_t(6, 1)
-    send_t(6, 1, 0)
-    got_t(2, 0)
-    send_t(2, 0, 1)
-    to_sib(6)
     fwd_b(1, 1)
-    to_sib(2)
-    got_sib(2)
-    got_sib(6)
-    weights(3, 2, 0)
-    transpose_texts(3, 2)
-    fwd_b(2, 1)
     got_t(5, 0)
     send_t(5, 0, 0)
     got_t(3, 1)
     send_t(3, 1, 1)
     fwd_b(3, 1)
     fwd_b(1, 0)
-    row(1)
+    got_sib(2)
+    got_sib(6)
+    weights(3, 2, 0)
     got_t(5, 1)
     to_sib(5)
     got_t(3, 0)
     to_sib(3)
+    transpose_texts(5, 3)
+    transpose_texts(3, 2)
+    transpose_images(0)
+    row(1)
     row(3)
     weights(5, 3, 1)
     weights(5, 3, 3)
@@ -300,18 +299,16 @@
     weights(3, 2, 3)
     transpose_images(1)
     transpose_images(3)
-    row(2)
-    weights(5, 3, 2)
-    weights(3, 2, 2)
-    transpose_images(2)
     got_t4()
     got_sib(3)
     got_sib(5)
     weights(0, 3, 0)
     weights(0, 3, 1)
-    weights(0, 3, 2)
     weights(0, 3, 3)
     transpose_texts(0, 3)
+    row(2)
+    weights(0, 8, 2)
+    transpose_images(2)
 
     def text_part(place, n):
         rows = slice(place * ROWS, (place + n) * ROWS)
@@ -439,10 +436,10 @@
 
     image_part(2, u_far)
     gb_far(2)
-    sib_part(0, 3)
     image_part(2, 1 - u_far)
     for ka in (1, 3, 0):
         gb_far(ka)
+    sib_part(0, 3)
     own_part(0, 3)
     got_part(0, 3)
     text_step(0, 0, 0)

time: 56.6 us -> 55.9 us (0.988)
  Pallas kernels: 53.2 us -> 52.4 us
    pallas_call x1, Pallas kernels: 53.2 us -> 52.4 us  [local(): pl.pallas_call(kernel, out_shape=(jax.ShapeDtypeStruct((PART, 1024), bf16...]
where the time goes in v4:
time: 55.9 us; the launch traced here: 55.7 us
  Pallas kernels  52.4 us (94%)
  between operations  1.93 us (3%)
  local copies, waits for them, and re-layouts  1.38 us (2%)
    pallas_call x1, Pallas kernels, local(): pl.pallas_call(kernel, out_shape=(jax.ShapeDtypeStruct((PART, 1024), bf16...  52.4 us
    unnamed x2, local copies, waits for them, and re-layouts  1.38 us

profile of v4, /device:TPU:1, one launch (start us, length us, event | category | flops | bytes accessed | tf_op | source)
XLA Modules:
  0.0 55.7 jit_solution(14567034574319745878)
XLA Ops:
  1.9 52.4 %shard_map.68 = (bf16[72,1024]{1,0:T(8,128)(2,1)S(1)}, f32[64,1152]{1,0:T(8,128)S(1)}) custom-call(bf16[64,1152]{1,0:T(8,128)(2,1)} %pic_hbm.1, bf16[64,1152]{1,0:T(8,128)(2,1)} %cap_hbm.1, s32[1,64]{1,0:T(1,128)} %bitcast.1, f32[1]{0:T(128)S(6)} %copy.9.mul, f32[1]{0:T(128)S(6)} %copy.10.shift), custom_call_target="tpu_custom_call" | custom-call | flops 7000000000 | bytes 1000000 | tf_op jit(solution)/shard_map/pallas_call | solution.py:514
  54.4 0.7 %copy.11 = bf16[72,1024]{1,0:T(8,128)(2,1)} copy(bf16[72,1024]{1,0:T(8,128)(2,1)S(1)} %get-tuple-element.4) | data formatting | bytes 294912
  55.0 0.7 %copy.12 = f32[64,1152]{1,0:T(8,128)} copy(f32[64,1152]{1,0:T(8,128)S(1)} %get-tuple-element.5) | data formatting | bytes 589824

commit v5 on v4

--- a/solution.py
+++ b/solution.py
@@ -40,7 +40,7 @@
 
 def kernel(pic_hbm, cap_hbm, lab_hbm, mul, shift, img_out, txt_out,
            pic, cap, lab, U, M, T, Ut, Tt, W, tacc, svec, own, sib_out, sib_in,
-           tstage, trecv, G, rbh, rbf, ra, ra_sib, r1, fin, ssem, rsem, lsem):
+           tstage, trecv, G, rbh, rbf, rbn, ra, ra_sib, r1, fin, ssem, rsem, lsem):
     batch = lax.axis_index("batch")
     group = lax.axis_index("group")
     z, yh = batch // 2, batch % 2
@@ -68,7 +68,7 @@
     sib = dev(x, y, z, 1 - core)
 
     loads = [pltpu.make_async_copy(src, dst, lsem.at[i]) for i, (src, dst) in enumerate(
-        ((pic_hbm, pic), (cap_hbm, cap), (lab_hbm, lab)))]
+        ((cap_hbm, cap), (pic_hbm, pic), (lab_hbm, lab)))]
     for load in loads:
         load.start()
     barrier = pltpu.get_barrier_semaphore()
@@ -94,10 +94,10 @@
         rdma(dst, dst, ssem.at[at(key)], rsem.at[at(key)], sib).wait_recv()
 
     me = slot(0, 0)
-    loads[1].wait()
+    loads[0].wait()
     t_unit, t_inv = unit_rows(cap[...])
     T[PLACE[0]] = t_unit.astype(bf16).reshape(2, HALF, D)
-    loads[0].wait()
+    loads[1].wait()
     p_unit, p_inv = unit_rows(pic[...])
     U[me] = p_unit.astype(bf16).reshape(2, HALF, D)
     pl.semaphore_wait(barrier, len(partners))
@@ -108,12 +108,11 @@
     def got_u(ka, kb, hf):
         got(("u", ka, kb, hf), U.at[slot(ka, kb), hf])
 
-    def send_m(ka, kb, da, db):
-        s = slot(ka, kb)
-        send(("m", (ka - da) % SIDE, (kb - db) % SIDE), M.at[s], M.at[s], plane(da, db))
-
-    def got_m(ka, kb):
-        got(("m", ka, kb), M.at[slot(ka, kb)])
+    def send_m(ka):
+        send(("m", SIDE - ka), M.at[me], M.at[me], plane(ka, 0))
+
+    def line(kb):
+        return M.at[pl.ds((pb + kb) % SIDE * SIDE, SIDE)]
 
     def send_t(k, hf, d):
         to = (k + (NZ - 1 if d == 0 else 1)) % NZ
@@ -152,8 +151,8 @@
     lane8 = lax.broadcasted_iota(jnp.int32, (8, 128), 1)
     meta = jnp.where(row8 == 0, inv_lane, jnp.where(row8 == 1, lab_lane, 0.0))
     M[me] = jnp.where(lane8 // ROWS == pa % 2, meta, 0.0)
-    for to in ((2, 0), (1, 0), (3, 0), (0, 2), (0, 1), (0, 3)):
-        send_m(0, 0, *to)
+    for ka in (2, 1, 3):
+        send_m(ka)
     to_sib(0)
     for step in (0, 1):
         for d in (0, 1):
@@ -173,20 +172,21 @@
         for d in ((0, 1) if hf == 0 else (1, 0)):
             send_u(ka, 0, hf, 0, (1, 3)[d])
 
-    def meta_b(ka):
-        got_m(ka, 0)
+    def meta_b():
+        for ka in (1, 3, 2):
+            got(("m", ka), M.at[slot(ka, 0)])
         for kb in (2, 1, 3):
-            send_m(ka, 0, 0, kb)
+            send(("ml", SIDE - kb), line(0), line(0), plane(0, kb))
 
     def row(kb):
+        if kb:
+            got(("ml", kb), line(kb))
         for ka in range(SIDE):
             if kb == 2:
                 got_u(ka, 2, 0)
                 got_u(ka, 2, 1)
             elif kb:
                 got_u(ka, kb, 1 if kb == 3 else 0)
-            if kb:
-                got_m(ka, kb)
 
     m = mul[0]
     shift0 = shift[0]
@@ -253,9 +253,7 @@
     fwd_b(0, 1)
     along_b(3, 1)
     along_b(1, 0)
-    meta_b(2)
-    meta_b(1)
-    meta_b(3)
+    meta_b()
     got_t(6, 0)
     send_t(6, 0, 0)
     got_t(2, 1)
@@ -353,19 +351,25 @@
         for d in (0, 1):
             send(("gh", ka, d), G.at[2, a_at(ka), d], rbh.at[ka, d], b_dev[d])
 
-    def gb_near(d, ka, fresh):
+    def gb_fresh(d):
         kb = (1, 3)[d]
-        hf = 1 - d if fresh else d
-        if not fresh:
-            got(("gh", ka, d), rbh.at[ka, d])
-            G[kb, a_at(ka), hf] = (G[kb, a_at(ka), hf].astype(f32) + rbh[ka, d].astype(f32)).astype(bf16)
-        send(("gf", ka, d, hf), G.at[kb, a_at(ka), hf], rbf.at[ka, d, hf], b_dev[d])
+        send(("gn", d), G.at[kb, :, 1 - d], rbn.at[d], b_dev[d])
+
+    def gb_near(d, ka):
+        kb = (1, 3)[d]
+        got(("gh", ka, d), rbh.at[ka, d])
+        G[kb, a_at(ka), d] = (G[kb, a_at(ka), d].astype(f32) + rbh[ka, d].astype(f32)).astype(bf16)
+        send(("gf", ka, d), G.at[kb, a_at(ka), d], rbf.at[ka, d], b_dev[d])
 
     def gb_sum(ka):
-        for d in (0, 1):
-            for hf in (0, 1):
-                got(("gf", ka, d, hf), rbf.at[ka, d, hf])
-        return G[0, a_at(ka)].astype(f32) + rbf[ka, 0].astype(f32) + rbf[ka, 1].astype(f32)
+        halves = []
+        for hf in (0, 1):
+            if ka == 2:
+                got(("gn", 1 - hf), rbn.at[1 - hf])
+            got(("gf", ka, hf), rbf.at[ka, hf])
+            halves.append(G[0, a_at(ka), hf].astype(f32) + rbf[ka, hf].astype(f32)
+                          + rbn[1 - hf, a_at(ka)].astype(f32))
+        return jnp.stack(halves)
 
     def text_sum(k, hf):
         p = PLACE[k]
@@ -447,14 +451,12 @@
     text_step(1, 0, 1)
     text_step(1, 1, 0)
     image_parts(1)
-    for ka in order:
-        gb_near(0, ka, True)
+    gb_fresh(0)
     image_parts(3)
-    for ka in order:
-        gb_near(1, ka, True)
+    gb_fresh(1)
     for ka in order:
         for d in (0, 1):
-            gb_near(d, ka, False)
+            gb_near(d, ka)
     text_step(1, 0, 0)
     text_step(1, 1, 1)
     sib_part(3, 5)
@@ -504,7 +506,8 @@
         pltpu.VMEM((2, 4, 2, HALF, D), bf16),
         pltpu.VMEM((4, 4, 2, FEAT, 256), bf16),
         pltpu.VMEM((4, 2, FEAT, 256), bf16),
-        pltpu.VMEM((4, 2, 2, FEAT, 256), bf16),
+        pltpu.VMEM((4, 2, FEAT, 256), bf16),
+        pltpu.VMEM((2, 4, FEAT, 256), bf16),
         pltpu.VMEM((2, 3, 2, PAD, 256), bf16),
         pltpu.VMEM((2, PAD, 256), bf16),
         pltpu.VMEM((4, 2, 2, PAD, 256), bf16),

time: 55.9 us -> 56.1 us (level)
  no operation moved by 1% of the time
where the time goes in v5:
time: 56.1 us; the launch traced here: 55.9 us
  Pallas kernels  52.6 us (94%)
  between operations  1.93 us (3%)
  local copies, waits for them, and re-layouts  1.38 us (2%)
    pallas_call x1, Pallas kernels, local(): pl.pallas_call(kernel, out_shape=(jax.ShapeDtypeStruct((PART, 1024), bf16...  52.6 us
    unnamed x2, local copies, waits for them, and re-layouts  1.38 us

profile of v5, /device:TPU:1, one launch (start us, length us, event | category | flops | bytes accessed | tf_op | source)
XLA Modules:
  0.0 55.9 jit_solution(15238627836239991805)
XLA Ops:
  1.9 52.6 %shard_map.68 = (bf16[72,1024]{1,0:T(8,128)(2,1)S(1)}, f32[64,1152]{1,0:T(8,128)S(1)}) custom-call(bf16[64,1152]{1,0:T(8,128)(2,1)} %pic_hbm.1, bf16[64,1152]{1,0:T(8,128)(2,1)} %cap_hbm.1, s32[1,64]{1,0:T(1,128)} %bitcast.1, f32[1]{0:T(128)S(6)} %copy.9.mul, f32[1]{0:T(128)S(6)} %copy.10.shift), custom_call_target="tpu_custom_call" | custom-call | flops 7000000000 | bytes 1000000 | tf_op jit(solution)/shard_map/pallas_call | solution.py:517
  54.6 0.7 %copy.11 = bf16[72,1024]{1,0:T(8,128)(2,1)} copy(bf16[72,1024]{1,0:T(8,128)(2,1)S(1)} %get-tuple-element.4) | data formatting | bytes 294912
  55.2 0.7 %copy.12 = f32[64,1152]{1,0:T(8,128)} copy(f32[64,1152]{1,0:T(8,128)S(1)} %get-tuple-element.5) | data formatting | bytes 589824
